TPU v7x, 32 devices: a whole 2x2x4 slice. The times are simulated.
32 devices in a mesh: rep: 4 (over z), table: 4 (over y, core), tensor: 2 (over x).
Axes of the slice: x: 2, y: 2, z: 4, core: 2. Of those that a mesh axis runs over, the one named last changes fastest.
Arguments:
- pooled: bfloat16 [128, 256, 192], P('rep', 'table'), may hold values from -6 to 6
- lc_weight: bfloat16 [256, 256], P('tensor'), may hold values from -0.375 to 0.375
- fm_proj: bfloat16 [256, 256], P(None, 'tensor'), may hold values from -0.375 to 0.375
- fm_out: bfloat16 [256, 192], P('tensor'), may hold values from -0.02734375 to 0.02734375
- cotangent: bfloat16 [128, 256, 192], P(('rep', 'table')), may hold values from -6 to 6
Outputs:
- layer_out: bfloat16 [128, 256, 192], P(('rep', 'table'))
- emb_grad: bfloat16 [128, 256, 192], P('rep', 'table', 'tensor')
- lc_grad: float32 [256, 256], P('tensor')
- proj_grad: float32 [256, 256], P(None, 'tensor')
- out_grad: float32 [256, 192], P('tensor')
All inputs are finite; a program needn't handle non-finite values.
Results may differ from a plain program's by a relative error of at most 0.015.
Values may be sent and summed in bfloat16 or wider, within the bound.
A program may use at most 64 MiB of HBM per device.

v0:
```python
import jax
import jax.numpy as jnp
from jax import lax
from jax.sharding import PartitionSpec as P


def quarter_terms(embeds, upstream, proj_part, out_part, lc_part, row_start):
    row_count = lc_part.shape[0]
    compressed = jnp.einsum(
        "snd,nk->sdk", embeds, proj_part, preferred_element_type=jnp.float32
    ).astype(jnp.bfloat16)
    interact = jnp.einsum(
        "snd,sdk->snk", embeds, compressed, preferred_element_type=jnp.float32
    ).astype(jnp.bfloat16)
    own_rows = lax.dynamic_slice_in_dim(embeds, row_start, row_count, 1)
    forward_term = jnp.einsum("snk,kd->snd", interact, out_part, preferred_element_type=jnp.float32)
    forward_term = forward_term + jnp.einsum(
        "sjd,jm->smd", own_rows, lc_part, preferred_element_type=jnp.float32
    )
    interact_grad = jnp.einsum(
        "snd,kd->snk", upstream, out_part, preferred_element_type=jnp.float32
    ).astype(jnp.bfloat16)
    compress_grad = jnp.einsum(
        "snd,snk->sdk", embeds, interact_grad, preferred_element_type=jnp.float32
    ).astype(jnp.bfloat16)
    input_grad = jnp.einsum(
        "snk,sdk->snd", interact_grad, compressed, preferred_element_type=jnp.float32
    )
    input_grad = input_grad + jnp.einsum(
        "nk,sdk->snd", proj_part, compress_grad, preferred_element_type=jnp.float32
    )
    lc_rows = jnp.einsum("jm,smd->sjd", lc_part, upstream, preferred_element_type=jnp.float32)
    lc_rows = lc_rows + lax.dynamic_slice_in_dim(upstream, row_start, row_count, 1).astype(
        jnp.float32
    )
    current = lax.dynamic_slice_in_dim(input_grad, row_start, row_count, 1)
    input_grad = lax.dynamic_update_slice_in_dim(input_grad, current + lc_rows, row_start, 1)
    out_term = jnp.einsum("snk,snd->kd", interact, upstream, preferred_element_type=jnp.float32)
    proj_term = jnp.einsum("snd,sdk->nk", embeds, compress_grad, preferred_element_type=jnp.float32)
    lc_term = jnp.einsum("sjd,smd->jm", own_rows, upstream, preferred_element_type=jnp.float32)
    return (forward_term, input_grad, out_term, proj_term, lc_term)


def feed_rows(pooled):
    embeds = lax.all_to_all(pooled, "table", split_axis=0, concat_axis=1, tiled=True)
    return embeds


def shards(pooled, lc_weight, fm_proj, fm_out, cotangent):
    tensor_index = lax.axis_index("tensor")
    table_count = lax.axis_size("table")
    sample_total = cotangent.shape[0] * lax.axis_size("rep") * table_count
    feature_width = cotangent.shape[2]
    emb_count = cotangent.shape[1]
    wide_scale = float(sample_total * feature_width) ** (-0.5)
    out_scale = float(sample_total * emb_count * feature_width) ** (-0.5)
    embeds = feed_rows(pooled)
    row_count = lc_weight.shape[0]
    forward_term, input_grad, out_term, proj_term, lc_term = quarter_terms(
        embeds, cotangent, fm_proj, fm_out, lc_weight, tensor_index * row_count
    )
    mixture = lax.psum(forward_term.astype(jnp.bfloat16), "tensor").astype(jnp.float32)
    layer_out = (embeds.astype(jnp.float32) + mixture).astype(jnp.bfloat16)
    out_grad, proj_grad, lc_grad = lax.psum(
        (out_term * out_scale, proj_term * wide_scale, lc_term * wide_scale), ("rep", "table")
    )
    reduced = lax.psum_scatter(
        input_grad.astype(jnp.bfloat16), "tensor", scatter_dimension=2, tiled=True
    )
    emb_grad = lax.all_to_all(reduced, "table", split_axis=1, concat_axis=0, tiled=True)
    return (layer_out, emb_grad, lc_grad, proj_grad, out_grad)


def solution(mesh):
    in_specs = (
        P("rep", "table", None),
        P("tensor", None),
        P(None, "tensor"),
        P("tensor", None),
        P(("rep", "table"), None, None),
    )
    out_specs = (
        P(("rep", "table"), None, None),
        P("rep", "table", "tensor"),
        P("tensor", None),
        P(None, "tensor"),
        P("tensor", None),
    )
    return jax.shard_map(shards, mesh=mesh, in_specs=in_specs, out_specs=out_specs, check_vma=False)
```

profile of v0, /device:TPU:0, one launch (start us, length us, event | category | flops | bytes accessed | tf_op | source)
XLA Modules:
  0.0 177.8 jit_solution(7585968797713927115)
XLA Ops:
  8.0 4.4 %all-to-all-start = ((bf16[32,64,192]{2,1,0:T(8,128)(2,1)}), bf16[32,64,192]{2,1,0:T(8,128)(2,1)S(1)}, u32[]{:S(2)}, u32[]{:S(2)}) async-start(bf16[32,64,192]{2,1,0:T(8,128)(2,1)} %param.5), calls=%async_computation | async-start | bytes 2097152 | tf_op jit(solution)/shard_map/all_to_all | solution.py:45
  12.4 0.5 convolution_convert_fusion
  12.9 14.0 %all-to-all-done = bf16[32,64,192]{2,1,0:T(8,128)(2,1)S(1)} async-done(((bf16[32,64,192]{2,1,0:T(8,128)(2,1)}), bf16[32,64,192]{2,1,0:T(8,128)(2,1)S(1)}, u32[]{:S(2)}, u32[]{:S(2)}) %all-to-all-start) | async-done | bytes 786464 | tf_op jit(solution)/shard_map/all_to_all | solution.py:45
  26.9 0.1 copy.38
  27.0 0.5 fusion.5
  27.5 0.2 copy-done.4
  27.7 1.3 convolution_convert_fusion.3
  29.0 1.4 fusion.21
  30.4 0.4 bitcast_add_fusion
  30.7 0.4 fusion.3
  31.1 1.0 convert_element_type.47
  32.2 0.0 all-reduce.6.cloned.1.call-start
  32.2 0.5 copy.39
  32.7 1.0 fusion.6
  33.7 1.5 fusion.4
  35.2 1.0 fusion.9
  36.3 1.1 fusion.8
  37.4 0.3 fusion.17
  37.8 0.0 all-reduce.6.cloned.1.call-update
  37.8 0.0 all-reduce.4.cloned.1.call-start
  37.8 1.2 fusion
  39.1 0.0 all-reduce.4.cloned.1.call-update
  39.1 11.7 %reduce-scatter.2.cloned.1.call-done = bf16[8,256,96]{1,2,0:T(8,128)(2,1)} async-done(((bf16[8,256,192]{1,2,0:T(8,128)(2,1)}), bf16[8,256,96]{1,2,0:T(8,128)(2,1)}) %reduce-scatter.2.cloned.1.call-update) | async-done | bytes 393232 | tf_op jit(solution)/shard_map/reduce_scatter | solution.py:67
  50.8 2.1 %copy.45 = bf16[8,256,96]{2,0,1:T(8,128)(2,1)} copy(bf16[8,256,96]{1,2,0:T(8,128)(2,1)} %reduce-scatter.2.cloned.1.call-done) | data formatting | bytes 786432 | tf_op jit(solution)/shard_map/reduce_scatter | solution.py:67
  52.8 3.5 %all-to-all-start.1 = ((bf16[8,256,96]{2,0,1:T(8,128)(2,1)}), bf16[8,256,96]{2,0,1:T(8,128)(2,1)S(1)}, u32[]{:S(2)}, u32[]{:S(2)}) async-start(bf16[8,256,96]{2,0,1:T(8,128)(2,1)} %copy.45), calls=%async_computation.2 | async-start | bytes 1048576 | tf_op jit(solution)/shard_map/all_to_all | solution.py:70
  56.3 72.2 %all-reduce.6.cloned.1.call-done = (f32[128,256]{1,0:T(8,128)}, f32[256,128]{0,1:T(8,128)}, f32[128,192]{0,1:T(8,128)}) async-done(((f32[128,256]{1,0:T(8,128)}, f32[256,128]{0,1:T(8,128)}, f32[128,192]{0,1:T(8,128)}), (f32[128,256]{1,0:T(8,128)}, f32[256,128]{0,1:T(8,128)}, f32[128,192]{0,1:T(8,128)})) %all-reduce.6.cloned.1.call-update) | async-done | bytes 360464 | tf_op jit(solution)/shard_map/psum | solution.py:64
  128.5 1.7 copy.50
  130.2 35.7 %all-reduce.4.cloned.1.call-done = bf16[8,256,192]{1,2,0:T(8,128)(2,1)} async-done(((bf16[8,256,192]{1,2,0:T(8,128)(2,1)}), bf16[8,256,192]{1,2,0:T(8,128)(2,1)}) %all-reduce.4.cloned.1.call-update) | async-done | bytes 786448 | tf_op jit(solution)/shard_map/psum | solution.py:62
  165.9 2.2 %add_convert_fusion = bf16[8,256,192]{1,2,0:T(8,128)(2,1)} fusion(bf16[8,256,192]{1,2,0:T(8,128)(2,1)} %all-reduce.4.cloned.1.call-done, bf16[8,256,192]{1,2,0:T(8,128)(2,1)S(1)} %copy.39), kind=kLoop, calls=%fused_computation.3 | loop fusion | flops 1572864 | bytes 2359296 | tf_op jit(solution)/shard_map/convert_element_type | solution.py:63
  168.1 0.9 copy.47
  169.0 0.7 copy.63
  169.7 0.6 copy.64
  (18 shorter events, 0.1 us)
Async XLA Ops:
  8.0 22.7 %copy-start = (bf16[128,256]{1,0:T(8,128)(2,1)S(1)}, bf16[128,256]{1,0:T(8,128)(2,1)}, u32[]{:S(2)}) copy-start(bf16[128,256]{1,0:T(8,128)(2,1)} %param.6) | copy-start | bytes 196612
  8.0 4.4 %copy-start.1 = (bf16[8,256,192]{1,2,0:T(8,128)(2,1)S(1)}, bf16[8,256,192]{1,2,0:T(8,128)(2,1)}, u32[]{:S(2)}) copy-start(bf16[8,256,192]{1,2,0:T(8,128)(2,1)} %param.9) | copy-start | bytes 2359300
  8.0 4.4 %copy-start.5 = (bf16[128,192]{0,1:T(8,128)(2,1)S(1)}, bf16[128,192]{0,1:T(8,128)(2,1)}, u32[]{:S(2)}) copy-start(bf16[128,192]{0,1:T(8,128)(2,1)} %param.8) | copy-start | bytes 147460
  8.0 18.8 %all-to-all-start = ((bf16[32,64,192]{2,1,0:T(8,128)(2,1)}), bf16[32,64,192]{2,1,0:T(8,128)(2,1)S(1)}, u32[]{:S(2)}, u32[]{:S(2)}) async-start(bf16[32,64,192]{2,1,0:T(8,128)(2,1)} %param.5), calls=%async_computation | async-start | bytes 2097152 | tf_op jit(solution)/shard_map/all_to_all | solution.py:45
  12.4 38.4 %reduce-scatter.2.cloned.1.call-start = ((), (), s32[]{:S(2)}) async-start(), calls=%async_computation.4 | async-start | bytes 1179648 | tf_op jit(solution)/shard_map/reduce_scatter | solution.py:67
  26.9 0.8 copy-start.4
  27.7 2.6 %copy-start.2 = (bf16[8,192,128]{2,1,0:T(8,128)(2,1)}, bf16[8,192,128]{2,1,0:T(8,128)(2,1)S(1)}, u32[]{:S(2)}) copy-start(bf16[8,192,128]{2,1,0:T(8,128)(2,1)S(1)} %fusion.5) | copy-start | bytes 1179652
  32.2 96.4 %all-reduce.6.cloned.1.call-start = ((), (), s32[]{:S(2)}) async-start(), calls=%async_computation.5 | async-start | bytes 720896 | tf_op jit(solution)/shard_map/psum | solution.py:64
  33.7 2.5 %copy-start.3 = (bf16[8,192,128]{2,1,0:T(8,128)(2,1)S(1)}, bf16[8,192,128]{2,1,0:T(8,128)(2,1)}, u32[]{:S(2)}) copy-start(bf16[8,192,128]{2,1,0:T(8,128)(2,1)} %copy-done.2) | copy-start | bytes 1179652
  37.8 128.1 %all-reduce.4.cloned.1.call-start = ((), (), s32[]{:S(2)}) async-start(), calls=%async_computation.3 | async-start | bytes 1572864 | tf_op jit(solution)/shard_map/psum | solution.py:62
  52.8 115.3 %all-to-all-start.1 = ((bf16[8,256,96]{2,0,1:T(8,128)(2,1)}), bf16[8,256,96]{2,0,1:T(8,128)(2,1)S(1)}, u32[]{:S(2)}, u32[]{:S(2)}) async-start(bf16[8,256,96]{2,0,1:T(8,128)(2,1)} %copy.45), calls=%async_computation.2 | async-start | bytes 1048576 | tf_op jit(solution)/shard_map/all_to_all | solution.py:70
  130.2 38.8 %copy-start.6 = (f32[128,256]{1,0:T(8,128)S(1)}, f32[128,256]{1,0:T(8,128)}, u32[]{:S(2)}) copy-start(f32[128,256]{1,0:T(8,128)} %get-tuple-element.30) | copy-start | bytes 393220
  130.2 39.5 %copy-start.7 = (f32[128,192]{0,1:T(8,128)S(1)}, f32[128,192]{0,1:T(8,128)}, u32[]{:S(2)}) copy-start(f32[128,192]{0,1:T(8,128)} %get-tuple-element.32) | copy-start | bytes 294916
Sparse Core Ops, SparseCore 0:
  32.3 18.4 reduce-scatter.1
Sparse Core Ops, SparseCore 1:
  37.9 90.6 all-reduce.5
  131.4 34.5 all-reduce.3
where the time goes:
time: 178 us
  waiting for transfers between devices  134 us (75%)
  between operations  15.6 us (9%)
  matrix products  10.6 us (6%)
  starting transfers between devices  7.94 us (4%)
  local copies, waits for them, and re-layouts  6.84 us (4%)
  other arithmetic  3.19 us (2%)
    psum x1, waiting for transfers between devices, shards(): lax.psum((out_term * out_scale, proj_term * wide_scale, lc_term * wide_sc...  72.2 us
    psum x1, waiting for transfers between devices, shards(): lax.psum(forward_term.astype(jnp.bfloat16), 'tensor').astype(jnp.float32)  35.7 us
    all_to_all x1, waiting for transfers between devices, feed_rows(): lax.all_to_all(pooled, 'table', split_axis=0, concat_axis=1, tiled=True)  14 us
    reduce_scatter x1, waiting for transfers between devices, shards(): lax.psum_scatter(input_grad.astype(jnp.bfloat16), 'tensor', scatter_dimen...  11.7 us
    all_to_all x1, starting transfers between devices, feed_rows(): lax.all_to_all(pooled, 'table', split_axis=0, concat_axis=1, tiled=True)  4.38 us
  transfers between devices with their start and end apart: 5, of which 4 were waited for; matrix products, arithmetic and copies ran while one was open for 7% of the time, Pallas kernels for 0%

commit v1 on v0

v1 whole, which is shorter than its diff:
```python
import functools

import jax
import jax.numpy as jnp
from jax import lax
from jax.experimental import pallas as pl
from jax.experimental.pallas import tpu as pltpu
from jax.sharding import PartitionSpec as P

MESH = pl.DeviceIdType.MESH
BF16 = jnp.bfloat16
F32 = jnp.float32


def dot_nn(a, b):
    return jnp.dot(a, b, preferred_element_type=F32)


def dot_nt(a, b):
    return lax.dot_general(a, b, (((1,), (1,)), ((), ())), preferred_element_type=F32)


def layer_kernel(cfg, pooled, lc_w, proj_w, out_w, cot, layer, emb, lc_g, proj_g, out_g, *scratch):
    (x_ref, g_ref, pw, ww, ow, pt, p_all, w_t, ct, cgt, lo, eg, acc_l, acc_p, acc_o,
     gb, rb1, sb, rb2, fs, loc, x_send, x_recv, w_send, w_recv, e_send, e_recv, r_send, r_recv) = scratch
    tables, reps, tensors = cfg["tables"], cfg["reps"], cfg["tensors"]
    samples, nr, n, d = cfg["samples"], cfg["nr"], cfg["n"], cfg["d"]
    kq, jq, dq, cs, pp, fused = cfg["kq"], cfg["jq"], cfg["dq"], cfg["cs"], cfg["pp"], cfg["fused"]
    chunks = samples // cs
    t = lax.axis_index("table")
    r = lax.axis_index("rep")
    x = lax.axis_index("tensor")

    def peer(axis, me, size, j):
        return {axis: lax.rem(me + j, size)}

    barrier = pltpu.get_barrier_semaphore()
    groups = [("table", t, tables), ("tensor", x, tensors)] + ([("rep", r, reps)] if fused else [])
    signals = 0
    for axis, me, size in groups:
        for j in range(1, size):
            pl.semaphore_signal(barrier, inc=1, device_id=peer(axis, me, size, j), device_id_type=MESH)
            signals += 1

    def g_load(c):
        rows = pl.ds(c * cs, cs)
        return pltpu.make_async_copy(cot.at[rows], g_ref.at[rows], loc.at[c])

    def x_load(c):
        return pltpu.make_async_copy(
            pooled.at[pl.ds(t * samples + c * cs, cs)], x_ref.at[pl.ds(c * cs, cs), t], loc.at[chunks + c]
        )

    w_pairs = ((proj_w, pw), (out_w, ow), (lc_w, ww))
    w_loads = [
        pltpu.make_async_copy(src, dst.at[x], loc.at[2 * chunks + i]) for i, (src, dst) in enumerate(w_pairs)
    ]
    for load in w_loads:
        load.start()
    for c in range(chunks):
        g_load(c).start()
        x_load(c).start()
    pl.semaphore_wait(barrier, signals)

    def x_copy(c, j):
        to = lax.rem(t + j, tables)
        return pltpu.make_async_remote_copy(
            pooled.at[pl.ds(to * samples + c * cs, cs)],
            x_ref.at[pl.ds(c * cs, cs), t],
            x_send.at[c, j - 1],
            x_recv.at[c, j - 1],
            device_id=peer("table", t, tables, j),
            device_id_type=MESH,
        )

    def w_copy(i, j):
        src, dst = w_pairs[i]
        return pltpu.make_async_remote_copy(
            src, dst.at[x], w_send.at[i, j - 1], w_recv.at[i, j - 1],
            device_id=peer("tensor", x, tensors, j), device_id_type=MESH,
        )

    for c in range(chunks):
        for j in range(1, tables):
            x_copy(c, j).start()
    for j in range(1, tensors):
        for i in range(3):
            w_copy(i, j).start()

    for load in w_loads:
        load.wait()
    pt[x] = pw[x].T
    acc_l[...] = jnp.zeros_like(acc_l)
    acc_p[...] = jnp.zeros_like(acc_p)
    acc_o[...] = jnp.zeros_like(acc_o)

    def first(c, carry):
        g_load(c).wait()
        x_load(c).wait()
        for j in range(1, tables):
            x_copy(c, j).wait_recv()
        own_pt, own_o = pt[x], ow[x]
        sum_l, sum_p, sum_o = acc_l[...], acc_p[...], acc_o[:, :d]
        for i in range(cs):
            s = c * cs + i
            xs = x_ref[s].reshape(n, d)
            gs = g_ref[s]
            own_rows = x_ref[s, pl.ds(x * (jq // nr), jq // nr)].reshape(jq, d)
            comp = dot_nn(own_pt, xs).astype(BF16)
            ct[s, x] = comp
            inter = dot_nt(comp, xs).astype(BF16)
            sum_o = sum_o + dot_nn(inter, gs)
            igrad = dot_nt(own_o, gs).astype(BF16)
            cgrad = dot_nn(igrad, xs).astype(BF16)
            cgt[s, x] = cgrad
            sum_p = sum_p + dot_nt(cgrad, xs)
            sum_l = sum_l + dot_nt(own_rows, gs)
        acc_l[...] = sum_l
        acc_p[...] = sum_p
        acc_o[:, :d] = sum_o
        return carry

    lax.fori_loop(0, chunks, first, 0)

    part = reps * pp

    def rs_table(j):
        to = lax.rem(t + j, tables)
        return pltpu.make_async_remote_copy(
            gb.at[pl.ds(to * part, part)], rb1.at[j - 1], r_send.at[0, j - 1], r_recv.at[0, j - 1],
            device_id=peer("table", t, tables, j), device_id_type=MESH,
        )

    def rs_rep(j):
        to = lax.rem(r + j, reps)
        return pltpu.make_async_remote_copy(
            sb.at[pl.ds(to * pp, pp)], rb2.at[j - 1], r_send.at[1, j - 1], r_recv.at[1, j - 1],
            device_id=peer("rep", r, reps, j), device_id_type=MESH,
        )

    def ag_rep(j):
        mine = fs.at[pl.ds(t * part + r * pp, pp)]
        return pltpu.make_async_remote_copy(
            mine, mine, r_send.at[2, j - 1], r_recv.at[2, j - 1],
            device_id=peer("rep", r, reps, j), device_id_type=MESH,
        )

    def ag_table(j):
        mine = fs.at[pl.ds(t * part, part)]
        return pltpu.make_async_remote_copy(
            mine, mine, r_send.at[3, j - 1], r_recv.at[3, j - 1],
            device_id=peer("table", t, tables, j), device_id_type=MESH,
        )

    halves = n // 128
    layout = ((acc_l, jq, cfg["wide_scale"]), (acc_p, kq, cfg["wide_scale"]), (acc_o, kq, cfg["out_scale"]))
    if fused:
        at = 0
        for ref, rows, scale in layout:
            for h in range(halves):
                value = (ref[:, h * 128:(h + 1) * 128] * scale).astype(BF16)
                gb[at:at + rows // 16] = value.reshape(rows // 16, 16, 128)
                at += rows // 16
        for j in range(1, tables):
            rs_table(j).start()

    def reduce_step(c):
        if not fused:
            return

        @pl.when(c == 0)
        def _():
            total = gb[pl.ds(t * part, part)].astype(F32)
            for j in range(1, tables):
                rs_table(j).wait_recv()
                total = total + rb1[j - 1].astype(F32)
            sb[...] = total.astype(BF16)
            for j in range(1, reps):
                rs_rep(j).start()

        @pl.when(c == 1)
        def _():
            total = sb[pl.ds(r * pp, pp)].astype(F32)
            for j in range(1, reps):
                rs_rep(j).wait_recv()
                total = total + rb2[j - 1].astype(F32)
            fs[pl.ds(t * part + r * pp, pp)] = total.astype(BF16)
            for j in range(1, reps):
                ag_rep(j).start()

        @pl.when(c == 2)
        def _():
            for j in range(1, reps):
                ag_rep(j).wait_recv()
            for j in range(1, tables):
                ag_table(j).start()

    for j in range(1, tensors):
        for i in range(3):
            w_copy(i, j).wait_recv()
    for j in range(1, tensors):
        q = lax.rem(x + j, tensors)
        pt[q] = pw[q].T
    p_all[...] = jnp.concatenate([pw[q] for q in range(tensors)], axis=1)
    w_t[...] = ww[...].reshape(n, n).T

    def lo_store(c):
        rows = pl.ds(c * cs, cs)
        return pltpu.make_async_copy(lo.at[rows], layer.at[rows], loc.at[2 * chunks + 3 + c])

    def e_store(c):
        return pltpu.make_async_copy(
            eg.at[pl.ds(c * cs, cs), t], emb.at[pl.ds(t * samples + c * cs, cs)], loc.at[3 * chunks + 3 + c]
        )

    def e_copy(c, j):
        to = lax.rem(t + j, tables)
        return pltpu.make_async_remote_copy(
            eg.at[pl.ds(c * cs, cs), to],
            emb.at[pl.ds(t * samples + c * cs, cs)],
            e_send.at[c, j - 1],
            e_recv.at[c, j - 1],
            device_id=peer("table", t, tables, j),
            device_id_type=MESH,
        )

    def second(c, carry):
        o_all = ow[...].reshape(tensors * kq, d)
        for i in range(cs):
            s = c * cs + i
            xs = x_ref[s].reshape(n, d)
            gs = g_ref[s]
            for j in range(1, tensors):
                q = lax.rem(x + j, tensors)
                ct[s, q] = dot_nn(pt[q], xs).astype(BF16)
                igrad_t = dot_nt(ow[q], gs).astype(BF16)
                cgt[s, q] = dot_nn(igrad_t, xs).astype(BF16)
            comp = ct[s].reshape(tensors * kq, d)
            cgrad = cgt[s].reshape(tensors * kq, d)
            igrad = dot_nt(gs, o_all).astype(BF16)
            grad = dot_nn(igrad, comp) + dot_nn(p_all[...], cgrad)
            grad = grad + dot_nn(ww[...].reshape(n, n), gs) + gs.astype(F32)
            own = grad[:, :dq]
            for q in range(1, tensors):
                own = jnp.where(x == q, grad[:, q * dq:(q + 1) * dq], own)
            eg[s] = own.reshape(tables, nr, dq).astype(BF16)
            inter = dot_nt(xs, comp).astype(BF16)
            mixture = dot_nn(inter, o_all) + dot_nn(w_t[...], xs)
            lo[s] = (xs.astype(F32) + mixture).astype(BF16)
        for j in range(1, tables):
            e_copy(c, j).start()
        e_store(c).start()
        lo_store(c).start()
        reduce_step(c)
        return carry

    lax.fori_loop(0, chunks, second, 0)

    if fused:
        for j in range(1, tables):
            ag_table(j).wait_recv()
        at = 0
        wide = []
        for ref, rows, scale in layout:
            pieces = []
            for h in range(halves):
                pieces.append(fs[at:at + rows // 16].reshape(rows, 128).astype(F32))
                at += rows // 16
            wide.append(pieces)
        lc_g[...] = jnp.concatenate(wide[0], axis=1)
        proj_g[...] = jnp.concatenate([piece.T for piece in wide[1]], axis=0)
        out_g[...] = jnp.concatenate(wide[2], axis=1)[:, :d]
    else:
        lc_g[...] = acc_l[...] * cfg["wide_scale"]
        proj_g[...] = (acc_p[...] * cfg["wide_scale"]).T
        out_g[...] = acc_o[:, :d] * cfg["out_scale"]

    for c in range(chunks):
        lo_store(c).wait()
        e_store(c).wait()
        for j in range(1, tables):
            e_copy(c, j).wait_recv()
    for c in range(chunks):
        for j in range(1, tables):
            x_copy(c, j).wait_send()
            e_copy(c, j).wait_send()
    for j in range(1, tensors):
        for i in range(3):
            w_copy(i, j).wait_send()
    if fused:
        for j in range(1, tables):
            rs_table(j).wait_send()
            ag_table(j).wait_send()
        for j in range(1, reps):
            rs_rep(j).wait_send()
            ag_rep(j).wait_send()


def shards(sizes, pooled, lc_weight, fm_proj, fm_out, cotangent):
    tables, reps, tensors = sizes["table"], sizes["rep"], sizes["tensor"]
    samples, n, d = cotangent.shape
    nr = pooled.shape[1]
    jq, kq, dq = lc_weight.shape[0], fm_out.shape[0], d // tensors
    total = samples * reps * tables
    cs = 2 if samples % 2 == 0 else 1
    chunks = samples // cs
    wide = -(-d // 128) * 128
    pieces = (n // 128) * (jq // 16 + kq // 16) + (wide // 128) * (kq // 16)
    group = tables * reps
    fused = pieces % group == 0 and wide == n and jq % 16 == 0 and kq % 16 == 0
    pp = pieces // group if fused else 1
    cfg = dict(
        tables=tables, reps=reps, tensors=tensors, samples=samples, nr=nr, n=n, d=d, kq=kq, jq=jq, dq=dq,
        cs=cs, pp=pp, fused=fused,
        wide_scale=float(total * d) ** (-0.5), out_scale=float(total * n * d) ** (-0.5),
    )
    part = reps * pp if fused else 1
    held = pieces if fused else 1
    dma = pltpu.SemaphoreType.DMA
    peers = max(tables - 1, 1)
    wpeers = max(tensors - 1, 1)
    rpeers = max(tables - 1, reps - 1, 1)
    scratch = [
        pltpu.VMEM((samples, tables, nr, d), BF16),
        pltpu.VMEM((samples, n, d), BF16),
        pltpu.VMEM((tensors, n, kq), BF16),
        pltpu.VMEM((tensors, jq, n), BF16),
        pltpu.VMEM((tensors, kq, d), BF16),
        pltpu.VMEM((tensors, kq, n), BF16),
        pltpu.VMEM((n, tensors * kq), BF16),
        pltpu.VMEM((n, n), BF16),
        pltpu.VMEM((samples, tensors, kq, d), BF16),
        pltpu.VMEM((samples, tensors, kq, d), BF16),
        pltpu.VMEM((samples, n, d), BF16),
        pltpu.VMEM((samples, tables, nr, dq), BF16),
        pltpu.VMEM((jq, n), F32),
        pltpu.VMEM((kq, n), F32),
        pltpu.VMEM((kq, wide), F32),
        pltpu.VMEM((held, 16, 128), BF16),
        pltpu.VMEM((peers, part, 16, 128), BF16),
        pltpu.VMEM((part, 16, 128), BF16),
        pltpu.VMEM((max(reps - 1, 1), pp, 16, 128), BF16),
        pltpu.VMEM((held, 16, 128), BF16),
        dma((4 * chunks + 3,)),
        dma((chunks, peers)),
        dma((chunks, peers)),
        dma((3, wpeers)),
        dma((3, wpeers)),
        dma((chunks, peers)),
        dma((chunks, peers)),
        dma((4, rpeers)),
        dma((4, rpeers)),
    ]
    hbm = pl.BlockSpec(memory_space=pl.ANY)
    vmem = pl.BlockSpec(memory_space=pltpu.VMEM)
    layer, emb, lc_g, proj_g, out_g = pl.pallas_call(
        functools.partial(layer_kernel, cfg),
        out_shape=(
            jax.ShapeDtypeStruct((samples, n, d), BF16),
            jax.ShapeDtypeStruct((pooled.shape[0], nr, dq), BF16),
            jax.ShapeDtypeStruct((jq, n), F32),
            jax.ShapeDtypeStruct((n, kq), F32),
            jax.ShapeDtypeStruct((kq, d), F32),
        ),
        in_specs=[hbm] * 5,
        out_specs=(hbm, hbm, vmem, vmem, vmem),
        scratch_shapes=scratch,
        compiler_params=pltpu.CompilerParams(
            collective_id=0, has_side_effects=True, vmem_limit_bytes=48 * 1024 * 1024
        ),
        name="interaction_layer",
    )(pooled, lc_weight, fm_proj, fm_out, cotangent)
    if not fused:
        lc_g, proj_g, out_g = lax.psum((lc_g, proj_g, out_g), ("rep", "table"))
    return layer, emb, lc_g, proj_g, out_g


def solution(mesh):
    in_specs = (
        P("rep", "table", None),
        P("tensor", None),
        P(None, "tensor"),
        P("tensor", None),
        P(("rep", "table"), None, None),
    )
    out_specs = (
        P(("rep", "table"), None, None),
        P("rep", "table", "tensor"),
        P("tensor", None),
        P(None, "tensor"),
        P("tensor", None),
    )
    return jax.shard_map(
        functools.partial(shards, dict(mesh.shape)),
        mesh=mesh, in_specs=in_specs, out_specs=out_specs, check_vma=False,
    )
```

time: 178 us -> 45.2 us (0.25)
  waiting for transfers between devices: 134 us -> 0 us
  Pallas kernels: 0 us -> 35.3 us
  between operations: 15.6 us -> 0.71 us
  matrix products: 10.6 us -> 0 us
  starting transfers between devices: 7.94 us -> 0 us
  other arithmetic: 3.19 us -> 0 us
  local copies, waits for them, and re-layouts: 6.84 us -> 9.06 us
    psum x2 -> x0, waiting for transfers between devices: 108 us -> none  [the longest x1 72.2 us: shards(): lax.psum((out_term * out_scale, proj_term * wide_scale, lc_term * wide_sc...]
    pallas_call x0 -> x1, Pallas kernels: none -> 35.3 us  [shards(): pl.pallas_call(functools.partial(layer_kernel, cfg), out_shape=(jax.Shape...]
    all_to_all x2 -> x0, waiting for transfers between devices: 14 us -> none  [the longest x1 14 us: feed_rows(): lax.all_to_all(pooled, 'table', split_axis=0, concat_axis=1, tiled=True)]
    reduce_scatter x1 -> x0, waiting for transfers between devices: 11.7 us -> none  [shards(): lax.psum_scatter(input_grad.astype(jnp.bfloat16), 'tensor', scatter_dimen...]
    dot_general x12 -> x0, matrix products: 10.6 us -> none  [the longest x1 1.53 us: quarter_terms(): jnp.einsum('snd,sdk->snk', embeds, compressed, preferred_element_type=jnp...]
    all_to_all x2 -> x0, starting transfers between devices: 7.85 us -> none  [the longest x1 4.38 us: feed_rows(): lax.all_to_all(pooled, 'table', split_axis=0, concat_axis=1, tiled=True)]
    unnamed x19, local copies, waits for them, and re-layouts: 3.22 us -> 7.07 us
    convert_element_type x2 -> x0, other arithmetic: 3.19 us -> none  [the longest x1 2.2 us: shards(): layer_out = (embeds.astype(jnp.float32) + mixture).astype(jnp.bfloat16)]
  transfers between devices with their start and end apart: 5 -> 0, of which waited for: 4 -> 0; matrix products, arithmetic and copies ran while one was open for 7% -> 0% of each run, Pallas kernels for 0% -> 0%
where the time goes in v1:
time: 45.2 us; the launch traced here: 45 us
  Pallas kernels  35.3 us (78%)
  local copies, waits for them, and re-layouts  9.06 us (20%)
  between operations  0.71 us (2%)
    pallas_call x1, Pallas kernels, shards(): pl.pallas_call(functools.partial(layer_kernel, cfg), out_shape=(jax.Shape...  35.3 us
    unnamed x19, local copies, waits for them, and re-layouts  7.07 us
    pallas_call x2, local copies, waits for them, and re-layouts, shards(): pl.pallas_call(functools.partial(layer_kernel, cfg), out_shape=(jax.Shape...  1.99 us

profile of v1, /device:TPU:0, one launch (start us, length us, event | category | flops | bytes accessed | tf_op | source)
XLA Modules:
  0.0 45.0 jit_solution(7585973429720758559)
XLA Ops:
  0.6 0.0 copy-start
  0.6 1.0 %copy.10.out_w = bf16[128,192]{1,0:T(8,128)(2,1)S(1)} copy(bf16[128,192]{0,1:T(8,128)(2,1)} %param.8) | data formatting | bytes 98304 | tf_op args[3]
  1.6 0.0 copy-start.5
  1.6 1.5 %copy.11.cot = bf16[8,256,192]{2,1,0:T(8,128)(2,1)S(1)} copy(bf16[8,256,192]{1,2,0:T(8,128)(2,1)} %param.9) | data formatting | bytes 1572864 | tf_op args[4]
  3.1 0.0 copy-done
  3.1 0.0 copy-done.5
  3.1 0.0 copy-start.6
  3.1 0.8 %copy-done.6 = bf16[256,128]{1,0:T(8,128)(2,1)S(1)} copy-done((bf16[256,128]{1,0:T(8,128)(2,1)S(1)}, bf16[256,128]{1,0:T(8,128)(2,1)}, u32[]{:S(2)}) %copy-start.6) | copy-done | bytes 65560
  4.0 35.3 %interaction_layer.1 = (bf16[8,256,192]{2,1,0:T(8,128)(2,1)S(1)}, bf16[32,64,96]{2,1,0:T(8,128)(2,1)S(1)}, f32[128,256]{1,0:T(8,128)S(1)}, f32[256,128]{1,0:T(8,128)S(1)}, f32[128,192]{1,0:T(8,128)S(1)}) custom-call(bf16[32,64,192]{2,1,0:T(8,128)(2,1)S(1)} %copy-done, bf16[128,256]{1,0:T(8,128)(2,1)S(1)} %copy-done.5, bf16[256,128]{1,0:T(8,128)(2,1)S(1)} %copy-done.6, ...), custom_call_target="tpu_custom_call" | custom-call | tf_op jit(solution)/shard_map/interaction_layer/pallas_call | solution.py:356
  39.2 0.0 copy-start.1
  39.3 0.8 %copy-done.1 = bf16[32,64,96]{2,1,0:T(8,128)(2,1)} copy-done((bf16[32,64,96]{2,1,0:T(8,128)(2,1)}, bf16[32,64,96]{2,1,0:T(8,128)(2,1)S(1)}, u32[]{:S(2)}) %copy-start.1) | copy-done | bytes 393240
  40.0 0.0 copy-start.3
  40.0 0.7 %copy-done.3 = f32[128,256]{1,0:T(8,128)} copy-done((f32[128,256]{1,0:T(8,128)}, f32[128,256]{1,0:T(8,128)S(1)}, u32[]{:S(2)}) %copy-start.3) | copy-done | bytes 131096
  40.7 0.0 copy-start.2
  40.7 1.3 %copy.12 = bf16[8,256,192]{1,2,0:T(8,128)(2,1)} copy(bf16[8,256,192]{2,1,0:T(8,128)(2,1)S(1)} %get-tuple-element.5) | data formatting | bytes 1572864 | tf_op jit(solution)/shard_map/interaction_layer/pallas_call | solution.py:356
  41.9 0.7 %copy.13 = f32[128,192]{0,1:T(8,128)} copy(f32[128,192]{1,0:T(8,128)S(1)} %get-tuple-element.9) | data formatting | bytes 196608 | tf_op jit(solution)/shard_map/interaction_layer/pallas_call | solution.py:356
  42.7 0.0 copy-done.2
  42.7 0.0 copy-start.4
  42.7 0.8 %copy.17 = bf16[32,64,96]{2,1,0:T(8,128)(2,1)} copy(bf16[32,64,96]{2,1,0:T(8,128)(2,1)S(1)} %copy-done.2) | data formatting | bytes 786432
  43.5 0.2 copy-done.4
  43.7 0.7 %copy.18 = f32[128,256]{1,0:T(8,128)} copy(f32[128,256]{1,0:T(8,128)S(1)} %copy-done.4) | data formatting | bytes 262144
  44.4 0.7 %copy.19 = f32[256,128]{1,0:T(8,128)} copy(f32[256,128]{1,0:T(8,128)S(1)} %get-tuple-element.18) | data formatting | bytes 262144
Async XLA Ops:
  0.6 2.5 %copy-start = (bf16[32,64,192]{2,1,0:T(8,128)(2,1)S(1)}, bf16[32,64,192]{2,1,0:T(8,128)(2,1)}, u32[]{:S(2)}) copy-start(bf16[32,64,192]{2,1,0:T(8,128)(2,1)} %pooled.1) | copy-start | bytes 2359300
  1.6 1.5 %copy-start.5 = (bf16[128,256]{1,0:T(8,128)(2,1)S(1)}, bf16[128,256]{1,0:T(8,128)(2,1)}, u32[]{:S(2)}) copy-start(bf16[128,256]{1,0:T(8,128)(2,1)} %lc_w.1) | copy-start | bytes 196612
  3.1 0.8 %copy-start.6 = (bf16[256,128]{1,0:T(8,128)(2,1)S(1)}, bf16[256,128]{1,0:T(8,128)(2,1)}, u32[]{:S(2)}) copy-start(bf16[256,128]{1,0:T(8,128)(2,1)} %proj_w.1) | copy-start | bytes 196612
  39.2 0.8 %copy-start.1 = (bf16[32,64,96]{2,1,0:T(8,128)(2,1)}, bf16[32,64,96]{2,1,0:T(8,128)(2,1)S(1)}, u32[]{:S(2)}) copy-start(bf16[32,64,96]{2,1,0:T(8,128)(2,1)S(1)} %get-tuple-element.16) | copy-start | bytes 1179652
  40.0 0.7 %copy-start.3 = (f32[128,256]{1,0:T(8,128)}, f32[128,256]{1,0:T(8,128)S(1)}, u32[]{:S(2)}) copy-start(f32[128,256]{1,0:T(8,128)S(1)} %get-tuple-element.17) | copy-start | bytes 393220
  40.7 2.0 %copy-start.2 = (bf16[32,64,96]{2,1,0:T(8,128)(2,1)S(1)}, bf16[32,64,96]{2,1,0:T(8,128)(2,1)}, u32[]{:S(2)}) copy-start(bf16[32,64,96]{2,1,0:T(8,128)(2,1)} %copy-done.1) | copy-start | bytes 1179652
  42.7 1.0 %copy-start.4 = (f32[128,256]{1,0:T(8,128)S(1)}, f32[128,256]{1,0:T(8,128)}, u32[]{:S(2)}) copy-start(f32[128,256]{1,0:T(8,128)} %copy-done.3) | copy-start | bytes 393220

commit v2 on v1

--- a/solution.py
+++ b/solution.py
@@ -10,22 +10,21 @@
 MESH = pl.DeviceIdType.MESH
 BF16 = jnp.bfloat16
 F32 = jnp.float32
+VMEM_BYTES = 60 * 1024 * 1024
 
 
 def dot_nn(a, b):
     return jnp.dot(a, b, preferred_element_type=F32)
 
 
-def dot_nt(a, b):
-    return lax.dot_general(a, b, (((1,), (1,)), ((), ())), preferred_element_type=F32)
-
-
-def layer_kernel(cfg, pooled, lc_w, proj_w, out_w, cot, layer, emb, lc_g, proj_g, out_g, *scratch):
-    (x_ref, g_ref, pw, ww, ow, pt, p_all, w_t, ct, cgt, lo, eg, acc_l, acc_p, acc_o,
-     gb, rb1, sb, rb2, fs, loc, x_send, x_recv, w_send, w_recv, e_send, e_recv, r_send, r_recv) = scratch
+def layer_kernel(cfg, pooled, lc_w, proj_w, out_w, cot, layer, emb, *rest):
     tables, reps, tensors = cfg["tables"], cfg["reps"], cfg["tensors"]
     samples, nr, n, d = cfg["samples"], cfg["nr"], cfg["n"], cfg["d"]
     kq, jq, dq, cs, pp, fused = cfg["kq"], cfg["jq"], cfg["dq"], cfg["cs"], cfg["pp"], cfg["fused"]
+    k = kq * tensors
+    grads, scratch = (rest[:1], rest[1:]) if fused else (rest[:3], rest[3:])
+    (x_ref, gt_ref, pw, ww, ow, pt, lhs, rhs, f_lhs, f_rhs, igt, lo, eg, acc_l, acc_p, acc_o,
+     gb, rb1, sb, rb2, fs, loc, x_send, x_recv, w_send, w_recv, e_send, e_recv, r_send, r_recv) = scratch
     chunks = samples // cs
     t = lax.axis_index("table")
     r = lax.axis_index("rep")
@@ -42,23 +41,21 @@
             pl.semaphore_signal(barrier, inc=1, device_id=peer(axis, me, size, j), device_id_type=MESH)
             signals += 1
 
-    def g_load(c):
-        rows = pl.ds(c * cs, cs)
-        return pltpu.make_async_copy(cot.at[rows], g_ref.at[rows], loc.at[c])
+    g_load = pltpu.make_async_copy(cot, gt_ref, loc.at[chunks])
 
     def x_load(c):
         return pltpu.make_async_copy(
-            pooled.at[pl.ds(t * samples + c * cs, cs)], x_ref.at[pl.ds(c * cs, cs), t], loc.at[chunks + c]
+            pooled.at[pl.ds(t * samples + c * cs, cs)], x_ref.at[pl.ds(c * cs, cs), t], loc.at[c]
         )
 
     w_pairs = ((proj_w, pw), (out_w, ow), (lc_w, ww))
     w_loads = [
-        pltpu.make_async_copy(src, dst.at[x], loc.at[2 * chunks + i]) for i, (src, dst) in enumerate(w_pairs)
+        pltpu.make_async_copy(src, dst.at[x], loc.at[chunks + 1 + i]) for i, (src, dst) in enumerate(w_pairs)
     ]
     for load in w_loads:
         load.start()
+    g_load.start()
     for c in range(chunks):
-        g_load(c).start()
         x_load(c).start()
     pl.semaphore_wait(barrier, signals)
 
@@ -90,31 +87,45 @@
     for load in w_loads:
         load.wait()
     pt[x] = pw[x].T
+    own_pt, own_o = pt[x], ow[x].T
     acc_l[...] = jnp.zeros_like(acc_l)
     acc_p[...] = jnp.zeros_like(acc_p)
     acc_o[...] = jnp.zeros_like(acc_o)
+    g_load.wait()
+
+    def block(q):
+        return pl.ds(pl.multiple_of(q * kq, kq), kq)
+
+    def before(c, carry):
+        for i in range(cs):
+            s = c * cs + i
+            gt = gt_ref[s]
+            rhs[s, 2 * k:] = gt.T
+            igt[s] = dot_nn(own_o, gt).astype(BF16)
+        return carry
+
+    lax.fori_loop(0, chunks, before, 0)
 
     def first(c, carry):
-        g_load(c).wait()
         x_load(c).wait()
         for j in range(1, tables):
             x_copy(c, j).wait_recv()
-        own_pt, own_o = pt[x], ow[x]
         sum_l, sum_p, sum_o = acc_l[...], acc_p[...], acc_o[:, :d]
         for i in range(cs):
             s = c * cs + i
             xs = x_ref[s].reshape(n, d)
-            gs = g_ref[s]
             own_rows = x_ref[s, pl.ds(x * (jq // nr), jq // nr)].reshape(jq, d)
+            xt = xs.T
+            f_lhs[s, :, k:] = xt
+            cgrad = dot_nn(igt[s], xs).astype(BF16)
+            rhs[s, pl.ds(pl.multiple_of(k + x * kq, kq), kq)] = cgrad
             comp = dot_nn(own_pt, xs).astype(BF16)
-            ct[s, x] = comp
-            inter = dot_nt(comp, xs).astype(BF16)
-            sum_o = sum_o + dot_nn(inter, gs)
-            igrad = dot_nt(own_o, gs).astype(BF16)
-            cgrad = dot_nn(igrad, xs).astype(BF16)
-            cgt[s, x] = cgrad
-            sum_p = sum_p + dot_nt(cgrad, xs)
-            sum_l = sum_l + dot_nt(own_rows, gs)
+            rhs[s, block(x)] = comp
+            inter = dot_nn(comp, xt).astype(BF16)
+            f_rhs[s, block(x)] = inter
+            sum_p = sum_p + dot_nn(cgrad, xt)
+            sum_l = sum_l + dot_nn(own_rows, gt_ref[s])
+            sum_o = sum_o + dot_nn(inter, rhs[s, 2 * k:])
         acc_l[...] = sum_l
         acc_p[...] = sum_p
         acc_o[:, :d] = sum_o
@@ -152,12 +163,11 @@
             device_id=peer("table", t, tables, j), device_id_type=MESH,
         )
 
-    halves = n // 128
     layout = ((acc_l, jq, cfg["wide_scale"]), (acc_p, kq, cfg["wide_scale"]), (acc_o, kq, cfg["out_scale"]))
     if fused:
         at = 0
         for ref, rows, scale in layout:
-            for h in range(halves):
+            for h in range(n // 128):
                 value = (ref[:, h * 128:(h + 1) * 128] * scale).astype(BF16)
                 gb[at:at + rows // 16] = value.reshape(rows // 16, 16, 128)
                 at += rows // 16
@@ -201,16 +211,22 @@
     for j in range(1, tensors):
         q = lax.rem(x + j, tensors)
         pt[q] = pw[q].T
-    p_all[...] = jnp.concatenate([pw[q] for q in range(tensors)], axis=1)
-    w_t[...] = ww[...].reshape(n, n).T
+    ot_all = jnp.concatenate([ow[q] for q in range(tensors)], axis=1)
+    w_all = ww[...].reshape(n, n)
+    for i in range(cs):
+        lhs[i, :, k:2 * k] = jnp.concatenate([pw[q] for q in range(tensors)], axis=1)
+        lhs[i, :, 2 * k:] = w_all
+    for s in range(samples):
+        f_lhs[s, :, :k] = ot_all
+        f_rhs[s, k:] = w_all
 
     def lo_store(c):
         rows = pl.ds(c * cs, cs)
-        return pltpu.make_async_copy(lo.at[rows], layer.at[rows], loc.at[2 * chunks + 3 + c])
+        return pltpu.make_async_copy(lo.at[rows], layer.at[rows], loc.at[chunks + 4 + c])
 
     def e_store(c):
         return pltpu.make_async_copy(
-            eg.at[pl.ds(c * cs, cs), t], emb.at[pl.ds(t * samples + c * cs, cs)], loc.at[3 * chunks + 3 + c]
+            eg.at[pl.ds(c * cs, cs), t], emb.at[pl.ds(t * samples + c * cs, cs)], loc.at[2 * chunks + 4 + c]
         )
 
     def e_copy(c, j):
@@ -225,28 +241,25 @@
         )
 
     def second(c, carry):
-        o_all = ow[...].reshape(tensors * kq, d)
         for i in range(cs):
             s = c * cs + i
             xs = x_ref[s].reshape(n, d)
-            gs = g_ref[s]
+            xt = f_lhs[s, :, k:]
+            gs = rhs[s, 2 * k:]
             for j in range(1, tensors):
                 q = lax.rem(x + j, tensors)
-                ct[s, q] = dot_nn(pt[q], xs).astype(BF16)
-                igrad_t = dot_nt(ow[q], gs).astype(BF16)
-                cgt[s, q] = dot_nn(igrad_t, xs).astype(BF16)
-            comp = ct[s].reshape(tensors * kq, d)
-            cgrad = cgt[s].reshape(tensors * kq, d)
-            igrad = dot_nt(gs, o_all).astype(BF16)
-            grad = dot_nn(igrad, comp) + dot_nn(p_all[...], cgrad)
-            grad = grad + dot_nn(ww[...].reshape(n, n), gs) + gs.astype(F32)
+                igrad_t = dot_nn(ow[q].T, gt_ref[s]).astype(BF16)
+                rhs[s, pl.ds(pl.multiple_of(k + q * kq, kq), kq)] = dot_nn(igrad_t, xs).astype(BF16)
+                comp = dot_nn(pt[q], xs).astype(BF16)
+                rhs[s, block(q)] = comp
+                f_rhs[s, block(q)] = dot_nn(comp, xt).astype(BF16)
+            lhs[i, :, :k] = dot_nn(gs, f_lhs[s, :, :k]).astype(BF16)
+            grad = dot_nn(lhs[i], rhs[s]) + gs.astype(F32)
             own = grad[:, :dq]
             for q in range(1, tensors):
                 own = jnp.where(x == q, grad[:, q * dq:(q + 1) * dq], own)
             eg[s] = own.reshape(tables, nr, dq).astype(BF16)
-            inter = dot_nt(xs, comp).astype(BF16)
-            mixture = dot_nn(inter, o_all) + dot_nn(w_t[...], xs)
-            lo[s] = (xs.astype(F32) + mixture).astype(BF16)
+            lo[s] = (dot_nn(f_lhs[s], f_rhs[s]) + xt.astype(F32)).astype(BF16)
         for j in range(1, tables):
             e_copy(c, j).start()
         e_store(c).start()
@@ -259,21 +272,10 @@
     if fused:
         for j in range(1, tables):
             ag_table(j).wait_recv()
-        at = 0
-        wide = []
-        for ref, rows, scale in layout:
-            pieces = []
-            for h in range(halves):
-                pieces.append(fs[at:at + rows // 16].reshape(rows, 128).astype(F32))
-                at += rows // 16
-            wide.append(pieces)
-        lc_g[...] = jnp.concatenate(wide[0], axis=1)
-        proj_g[...] = jnp.concatenate([piece.T for piece in wide[1]], axis=0)
-        out_g[...] = jnp.concatenate(wide[2], axis=1)[:, :d]
+        grads[0][...] = fs[...]
     else:
-        lc_g[...] = acc_l[...] * cfg["wide_scale"]
-        proj_g[...] = (acc_p[...] * cfg["wide_scale"]).T
-        out_g[...] = acc_o[:, :d] * cfg["out_scale"]
+        for ref, (acc, rows, scale) in zip(grads, layout):
+            ref[...] = acc[:, :ref.shape[1]] * scale
 
     for c in range(chunks):
         lo_store(c).wait()
@@ -294,6 +296,28 @@
         for j in range(1, reps):
             rs_rep(j).wait_send()
             ag_rep(j).wait_send()
+
+
+def write_kernel(layer, emb, pieces, layer_out, emb_out, lc_g, proj_g, out_g, sems):
+    copies = [
+        pltpu.make_async_copy(src, dst, sems.at[i])
+        for i, (src, dst) in enumerate(((layer, layer_out), (emb, emb_out)))
+    ]
+    for copy in copies:
+        copy.start()
+    at = 0
+    wide = []
+    for rows in (lc_g.shape[0], proj_g.shape[1], out_g.shape[1]):
+        halves = []
+        for _ in range(lc_g.shape[1] // 128):
+            halves.append(pieces[at:at + rows // 16].reshape(rows, 128).astype(F32))
+            at += rows // 16
+        wide.append(halves)
+    lc_g[...] = jnp.concatenate(wide[0], axis=1)
+    proj_g[...] = jnp.concatenate([half.T for half in wide[1]], axis=0)
+    out_g[...] = jnp.concatenate([half.T for half in wide[2]], axis=0)[:out_g.shape[0]]
+    for copy in copies:
+        copy.wait()
 
 
 def shards(sizes, pooled, lc_weight, fm_proj, fm_out, cotangent):
@@ -320,18 +344,20 @@
     peers = max(tables - 1, 1)
     wpeers = max(tensors - 1, 1)
     rpeers = max(tables - 1, reps - 1, 1)
+    k = kq * tensors
     scratch = [
         pltpu.VMEM((samples, tables, nr, d), BF16),
-        pltpu.VMEM((samples, n, d), BF16),
+        pltpu.VMEM((samples, d, n), BF16),
         pltpu.VMEM((tensors, n, kq), BF16),
         pltpu.VMEM((tensors, jq, n), BF16),
-        pltpu.VMEM((tensors, kq, d), BF16),
+        pltpu.VMEM((tensors, d, kq), BF16),
         pltpu.VMEM((tensors, kq, n), BF16),
-        pltpu.VMEM((n, tensors * kq), BF16),
-        pltpu.VMEM((n, n), BF16),
-        pltpu.VMEM((samples, tensors, kq, d), BF16),
-        pltpu.VMEM((samples, tensors, kq, d), BF16),
-        pltpu.VMEM((samples, n, d), BF16),
+        pltpu.VMEM((cs, n, 2 * k + n), BF16),
+        pltpu.VMEM((samples, 2 * k + n, d), BF16),
+        pltpu.VMEM((samples, d, k + n), BF16),
+        pltpu.VMEM((samples, k + n, n), BF16),
+        pltpu.VMEM((samples, kq, n), BF16),
+        pltpu.VMEM((samples, d, n), BF16),
         pltpu.VMEM((samples, tables, nr, dq), BF16),
         pltpu.VMEM((jq, n), F32),
         pltpu.VMEM((kq, n), F32),
@@ -341,7 +367,7 @@
         pltpu.VMEM((part, 16, 128), BF16),
         pltpu.VMEM((max(reps - 1, 1), pp, 16, 128), BF16),
         pltpu.VMEM((held, 16, 128), BF16),
-        dma((4 * chunks + 3,)),
+        dma((3 * chunks + 4,)),
         dma((chunks, peers)),
         dma((chunks, peers)),
         dma((3, wpeers)),
@@ -353,26 +379,44 @@
     ]
     hbm = pl.BlockSpec(memory_space=pl.ANY)
     vmem = pl.BlockSpec(memory_space=pltpu.VMEM)
-    layer, emb, lc_g, proj_g, out_g = pl.pallas_call(
+    layer_shape = jax.ShapeDtypeStruct((samples, d, n), BF16)
+    emb_shape = jax.ShapeDtypeStruct((pooled.shape[0], nr, dq), BF16)
+    if fused:
+        grad_shapes = (jax.ShapeDtypeStruct((pieces, 16, 128), BF16),)
+    else:
+        grad_shapes = tuple(jax.ShapeDtypeStruct(s, F32) for s in ((jq, n), (kq, n), (kq, d)))
+    layer, emb, *grads = pl.pallas_call(
         functools.partial(layer_kernel, cfg),
-        out_shape=(
-            jax.ShapeDtypeStruct((samples, n, d), BF16),
-            jax.ShapeDtypeStruct((pooled.shape[0], nr, dq), BF16),
-            jax.ShapeDtypeStruct((jq, n), F32),
-            jax.ShapeDtypeStruct((n, kq), F32),
-            jax.ShapeDtypeStruct((kq, d), F32),
-        ),
+        out_shape=(layer_shape, emb_shape, *grad_shapes),
         in_specs=[hbm] * 5,
-        out_specs=(hbm, hbm, vmem, vmem, vmem),
+        out_specs=(hbm, hbm) + (vmem,) * len(grad_shapes),
         scratch_shapes=scratch,
         compiler_params=pltpu.CompilerParams(
-            collective_id=0, has_side_effects=True, vmem_limit_bytes=48 * 1024 * 1024
+            collective_id=0, has_side_effects=True, vmem_limit_bytes=VMEM_BYTES
         ),
         name="interaction_layer",
-    )(pooled, lc_weight, fm_proj, fm_out, cotangent)
-    if not fused:
-        lc_g, proj_g, out_g = lax.psum((lc_g, proj_g, out_g), ("rep", "table"))
-    return layer, emb, lc_g, proj_g, out_g
+    )(pooled, lc_weight, fm_proj, fm_out.T, cotangent.transpose(0, 2, 1))
+    if fused:
+        layer, emb, lc_g, proj_g, out_t = pl.pallas_call(
+            write_kernel,
+            out_shape=(
+                layer_shape,
+                emb_shape,
+                jax.ShapeDtypeStruct((jq, n), F32),
+                jax.ShapeDtypeStruct((n, kq), F32),
+                jax.ShapeDtypeStruct((d, kq), F32),
+            ),
+            in_specs=[hbm, hbm, vmem],
+            out_specs=(hbm, hbm, vmem, vmem, vmem),
+            scratch_shapes=[dma((2,))],
+            compiler_params=pltpu.CompilerParams(vmem_limit_bytes=VMEM_BYTES),
+            name="write_outputs",
+        )(layer, emb, *grads)
+        out_g = out_t.T
+    else:
+        lc_g, proj_t, out_g = lax.psum(tuple(grads), ("rep", "table"))
+        proj_g = proj_t.T
+    return layer.transpose(0, 2, 1), emb, lc_g, proj_g, out_g
 
 
 def solution(mesh):

time: 45.2 us -> 79.3 us (1.75)
  Pallas kernels: 35.3 us -> 78.5 us
  local copies, waits for them, and re-layouts: 9.06 us -> 0 us
    pallas_call x1 -> x2, Pallas kernels: 35.3 us -> 78.5 us  [the longest x1 42.5 us: shards(): pl.pallas_call(write_kernel, out_shape=(layer_shape, emb_shape, jax.Shape...]
    unnamed x19 -> x0, local copies, waits for them, and re-layouts: 7.07 us -> none
    pallas_call x2 -> x0, local copies, waits for them, and re-layouts: 1.99 us -> none  [shards(): pl.pallas_call(functools.partial(layer_kernel, cfg), out_shape=(jax.Shape...]
where the time goes in v2:
time: 79.3 us; the launch traced here: 79.1 us
  Pallas kernels  78.5 us (99%)
    pallas_call x1, Pallas kernels, shards(): pl.pallas_call(write_kernel, out_shape=(layer_shape, emb_shape, jax.Shape...  42.5 us
    pallas_call x1, Pallas kernels, shards(): pl.pallas_call(functools.partial(layer_kernel, cfg), out_shape=(layer_sha...  36 us

profile of v2, /device:TPU:0, one launch (start us, length us, event | category | flops | bytes accessed | tf_op | source)
XLA Modules:
  0.0 79.1 jit_solution(8387670908765096896)
XLA Ops:
  0.6 36.0 %interaction_layer.1 = (bf16[8,192,256]{2,1,0:T(8,128)(2,1)}, bf16[32,64,96]{2,1,0:T(8,128)(2,1)}, bf16[48,16,128]{2,1,0:T(8,128)(2,1)}) custom-call(bf16[32,64,192]{2,1,0:T(8,128)(2,1)} %pooled.1, bf16[128,256]{1,0:T(8,128)(2,1)} %lc_w.1, bf16[256,128]{1,0:T(8,128)(2,1)} %proj_w.1, bf16[192,128]{1,0:T(8,128)(2,1)} %bitcast.5, bf16[8,192,256]{2,1,0:T(8,128)(2,1)} %bitcast.4), custom_call_target="tpu_custom_call" | custom-call | tf_op jit(solution)/shard_map/interaction_layer/pallas_call | solution.py:388
  36.7 42.5 %write_outputs.1 = (bf16[8,192,256]{2,1,0:T(8,128)(2,1)}, bf16[32,64,96]{2,1,0:T(8,128)(2,1)}, f32[128,256]{1,0:T(8,128)}, f32[256,128]{1,0:T(8,128)}, f32[192,128]{1,0:T(8,128)}) custom-call(bf16[8,192,256]{2,1,0:T(8,128)(2,1)} %get-tuple-element.13.layer, bf16[32,64,96]{2,1,0:T(8,128)(2,1)} %get-tuple-element.14.emb, ...), custom_call_target="tpu_custom_call" | custom-call | tf_op jit(solution)/shard_map/write_outputs/pallas_call | solution.py:400

commit v3 on v2

--- a/solution.py
+++ b/solution.py
@@ -21,9 +21,8 @@
     tables, reps, tensors = cfg["tables"], cfg["reps"], cfg["tensors"]
     samples, nr, n, d = cfg["samples"], cfg["nr"], cfg["n"], cfg["d"]
     kq, jq, dq, cs, pp, fused = cfg["kq"], cfg["jq"], cfg["dq"], cfg["cs"], cfg["pp"], cfg["fused"]
-    k = kq * tensors
     grads, scratch = (rest[:1], rest[1:]) if fused else (rest[:3], rest[3:])
-    (x_ref, gt_ref, pw, ww, ow, pt, lhs, rhs, f_lhs, f_rhs, igt, lo, eg, acc_l, acc_p, acc_o,
+    (x_ref, gt_ref, g_ref, xt_ref, pw, ww, ow, p_rel, ot_rel, own_ct, own_cgt, own_it, igt, lo, eg, acc_l, acc_p, acc_o,
      gb, rb1, sb, rb2, fs, loc, x_send, x_recv, w_send, w_recv, e_send, e_recv, r_send, r_recv) = scratch
     chunks = samples // cs
     t = lax.axis_index("table")
@@ -86,21 +85,17 @@
 
     for load in w_loads:
         load.wait()
-    pt[x] = pw[x].T
-    own_pt, own_o = pt[x], ow[x].T
+    own_pt, own_o = pw[x].T, ow[x].T
     acc_l[...] = jnp.zeros_like(acc_l)
     acc_p[...] = jnp.zeros_like(acc_p)
     acc_o[...] = jnp.zeros_like(acc_o)
     g_load.wait()
 
-    def block(q):
-        return pl.ds(pl.multiple_of(q * kq, kq), kq)
-
     def before(c, carry):
-        for i in range(cs):
-            s = c * cs + i
+        at = [c * cs + i for i in range(cs)]
+        for s in at:
             gt = gt_ref[s]
-            rhs[s, 2 * k:] = gt.T
+            g_ref[s] = gt.T
             igt[s] = dot_nn(own_o, gt).astype(BF16)
         return carry
 
@@ -110,25 +105,30 @@
         x_load(c).wait()
         for j in range(1, tables):
             x_copy(c, j).wait_recv()
-        sum_l, sum_p, sum_o = acc_l[...], acc_p[...], acc_o[:, :d]
-        for i in range(cs):
-            s = c * cs + i
-            xs = x_ref[s].reshape(n, d)
-            own_rows = x_ref[s, pl.ds(x * (jq // nr), jq // nr)].reshape(jq, d)
-            xt = xs.T
-            f_lhs[s, :, k:] = xt
-            cgrad = dot_nn(igt[s], xs).astype(BF16)
-            rhs[s, pl.ds(pl.multiple_of(k + x * kq, kq), kq)] = cgrad
-            comp = dot_nn(own_pt, xs).astype(BF16)
-            rhs[s, block(x)] = comp
-            inter = dot_nn(comp, xt).astype(BF16)
-            f_rhs[s, block(x)] = inter
-            sum_p = sum_p + dot_nn(cgrad, xt)
-            sum_l = sum_l + dot_nn(own_rows, gt_ref[s])
-            sum_o = sum_o + dot_nn(inter, rhs[s, 2 * k:])
+        at = [c * cs + i for i in range(cs)]
+        own_rows = [x_ref[s, pl.ds(x * (jq // nr), jq // nr)].reshape(jq, d) for s in at]
+        xs = [x_ref[s].reshape(n, d) for s in at]
+        xt = [v.T for v in xs]
+        comp = [dot_nn(own_pt, v).astype(BF16) for v in xs]
+        cgrad = [dot_nn(igt[s], v).astype(BF16) for s, v in zip(at, xs)]
+        sum_l = acc_l[...]
+        for s, v in zip(at, own_rows):
+            sum_l = sum_l + dot_nn(v, gt_ref[s])
+        inter = [dot_nn(v, w).astype(BF16) for v, w in zip(comp, xt)]
+        sum_p = acc_p[...]
+        for v, w in zip(cgrad, xt):
+            sum_p = sum_p + dot_nn(v, w)
+        sum_o = acc_o[:, :d]
+        for s, v in zip(at, inter):
+            sum_o = sum_o + dot_nn(v, g_ref[s])
         acc_l[...] = sum_l
         acc_p[...] = sum_p
         acc_o[:, :d] = sum_o
+        for i, s in enumerate(at):
+            xt_ref[s] = xt[i]
+            own_ct[s] = comp[i]
+            own_cgt[s] = cgrad[i]
+            own_it[s] = inter[i]
         return carry
 
     lax.fori_loop(0, chunks, first, 0)
@@ -208,17 +208,11 @@
     for j in range(1, tensors):
         for i in range(3):
             w_copy(i, j).wait_recv()
-    for j in range(1, tensors):
-        q = lax.rem(x + j, tensors)
-        pt[q] = pw[q].T
-    ot_all = jnp.concatenate([ow[q] for q in range(tensors)], axis=1)
-    w_all = ww[...].reshape(n, n)
-    for i in range(cs):
-        lhs[i, :, k:2 * k] = jnp.concatenate([pw[q] for q in range(tensors)], axis=1)
-        lhs[i, :, 2 * k:] = w_all
-    for s in range(samples):
-        f_lhs[s, :, :k] = ot_all
-        f_rhs[s, k:] = w_all
+    order = [x] + [lax.rem(x + j, tensors) for j in range(1, tensors)]
+    p_rel[...] = jnp.concatenate([pw[q] for q in order], axis=1)
+    ot_rel[...] = jnp.concatenate([ow[q] for q in order], axis=1)
+    other_pt = [pw[q].T for q in order[1:]]
+    other_o = [ow[q].T for q in order[1:]]
 
     def lo_store(c):
         rows = pl.ds(c * cs, cs)
@@ -241,28 +235,31 @@
         )
 
     def second(c, carry):
-        for i in range(cs):
-            s = c * cs + i
-            xs = x_ref[s].reshape(n, d)
-            xt = f_lhs[s, :, k:]
-            gs = rhs[s, 2 * k:]
-            for j in range(1, tensors):
-                q = lax.rem(x + j, tensors)
-                igrad_t = dot_nn(ow[q].T, gt_ref[s]).astype(BF16)
-                rhs[s, pl.ds(pl.multiple_of(k + q * kq, kq), kq)] = dot_nn(igrad_t, xs).astype(BF16)
-                comp = dot_nn(pt[q], xs).astype(BF16)
-                rhs[s, block(q)] = comp
-                f_rhs[s, block(q)] = dot_nn(comp, xt).astype(BF16)
-            lhs[i, :, :k] = dot_nn(gs, f_lhs[s, :, :k]).astype(BF16)
-            grad = dot_nn(lhs[i], rhs[s]) + gs.astype(F32)
+        at = [c * cs + i for i in range(cs)]
+        xs = [x_ref[s].reshape(n, d) for s in at]
+        w_all = ww[...].reshape(n, n)
+        igrad_t = [[dot_nn(v, gt_ref[s]).astype(BF16) for v in other_o] for s in at]
+        comp = [[dot_nn(v, w).astype(BF16) for v in other_pt] for w in xs]
+        igrad = [dot_nn(g_ref[s], ot_rel[...]).astype(BF16) for s in at]
+        cgrad = [[dot_nn(v, w).astype(BF16) for v in vs] for vs, w in zip(igrad_t, xs)]
+        inter = [[dot_nn(v, xt_ref[s]).astype(BF16) for v in vs] for vs, s in zip(comp, at)]
+        for i, s in enumerate(at):
+            gs = g_ref[s]
+            left = jnp.concatenate([igrad[i], p_rel[...], w_all], axis=1)
+            right = jnp.concatenate([own_ct[s], *comp[i], own_cgt[s], *cgrad[i], gs], axis=0)
+            grad = dot_nn(left, right) + gs.astype(F32)
             own = grad[:, :dq]
             for q in range(1, tensors):
                 own = jnp.where(x == q, grad[:, q * dq:(q + 1) * dq], own)
             eg[s] = own.reshape(tables, nr, dq).astype(BF16)
-            lo[s] = (dot_nn(f_lhs[s], f_rhs[s]) + xt.astype(F32)).astype(BF16)
         for j in range(1, tables):
             e_copy(c, j).start()
         e_store(c).start()
+        for i, s in enumerate(at):
+            xt = xt_ref[s]
+            left = jnp.concatenate([ot_rel[...], xt], axis=1)
+            right = jnp.concatenate([own_it[s], *inter[i], w_all], axis=0)
+            lo[s] = (dot_nn(left, right) + xt.astype(F32)).astype(BF16)
         lo_store(c).start()
         reduce_step(c)
         return carry
@@ -298,13 +295,21 @@
             ag_rep(j).wait_send()
 
 
-def write_kernel(layer, emb, pieces, layer_out, emb_out, lc_g, proj_g, out_g, sems):
-    copies = [
-        pltpu.make_async_copy(src, dst, sems.at[i])
-        for i, (src, dst) in enumerate(((layer, layer_out), (emb, emb_out)))
-    ]
-    for copy in copies:
-        copy.start()
+def write_kernel(layer, emb, pieces, layer_out, emb_out, lc_g, proj_g, out_g, held_l, held_e, sems):
+    loads, stores = [], []
+    for src, held, dst in ((layer, held_l, layer_out), (emb, held_e, emb_out)):
+        parts = 4 if src.shape[0] % 4 == 0 else 1
+        size = src.shape[0] // parts
+        for p in range(parts):
+            rows = pl.ds(p * size, size)
+            at = len(loads)
+            loads.append(pltpu.make_async_copy(src.at[rows], held.at[rows], sems.at[0, at]))
+            stores.append(pltpu.make_async_copy(held.at[rows], dst.at[rows], sems.at[1, at]))
+    for load in loads:
+        load.start()
+    for load, store in zip(loads, stores):
+        load.wait()
+        store.start()
     at = 0
     wide = []
     for rows in (lc_g.shape[0], proj_g.shape[1], out_g.shape[1]):
@@ -316,8 +321,8 @@
     lc_g[...] = jnp.concatenate(wide[0], axis=1)
     proj_g[...] = jnp.concatenate([half.T for half in wide[1]], axis=0)
     out_g[...] = jnp.concatenate([half.T for half in wide[2]], axis=0)[:out_g.shape[0]]
-    for copy in copies:
-        copy.wait()
+    for store in stores:
+        store.wait()
 
 
 def shards(sizes, pooled, lc_weight, fm_proj, fm_out, cotangent):
@@ -348,14 +353,16 @@
     scratch = [
         pltpu.VMEM((samples, tables, nr, d), BF16),
         pltpu.VMEM((samples, d, n), BF16),
+        pltpu.VMEM((samples, n, d), BF16),
+        pltpu.VMEM((samples, d, n), BF16),
         pltpu.VMEM((tensors, n, kq), BF16),
         pltpu.VMEM((tensors, jq, n), BF16),
         pltpu.VMEM((tensors, d, kq), BF16),
-        pltpu.VMEM((tensors, kq, n), BF16),
-        pltpu.VMEM((cs, n, 2 * k + n), BF16),
-        pltpu.VMEM((samples, 2 * k + n, d), BF16),
-        pltpu.VMEM((samples, d, k + n), BF16),
-        pltpu.VMEM((samples, k + n, n), BF16),
+        pltpu.VMEM((n, k), BF16),
+        pltpu.VMEM((d, k), BF16),
+        pltpu.VMEM((samples, kq, d), BF16),
+        pltpu.VMEM((samples, kq, d), BF16),
+        pltpu.VMEM((samples, kq, n), BF16),
         pltpu.VMEM((samples, kq, n), BF16),
         pltpu.VMEM((samples, d, n), BF16),
         pltpu.VMEM((samples, tables, nr, dq), BF16),
@@ -408,7 +415,9 @@
             ),
             in_specs=[hbm, hbm, vmem],
             out_specs=(hbm, hbm, vmem, vmem, vmem),
-            scratch_shapes=[dma((2,))],
+            scratch_shapes=[
+                pltpu.VMEM(layer_shape.shape, BF16), pltpu.VMEM(emb_shape.shape, BF16), dma((2, 8)),
+            ],
             compiler_params=pltpu.CompilerParams(vmem_limit_bytes=VMEM_BYTES),
             name="write_outputs",
         )(layer, emb, *grads)

time: 79.3 us -> 40.3 us (0.51)
  Pallas kernels: 78.5 us -> 39.5 us
    pallas_call x1, Pallas kernels: 42.5 us -> 3.86 us  [shards(): pl.pallas_call(write_kernel, out_shape=(layer_shape, emb_shape, jax.Shape...]
where the time goes in v3:
time: 40.3 us; the launch traced here: 40.1 us
  Pallas kernels  39.5 us (98%)
  between operations  0.64 us (2%)
    pallas_call x1, Pallas kernels, shards(): pl.pallas_call(functools.partial(layer_kernel, cfg), out_shape=(layer_sha...  35.6 us
    pallas_call x1, Pallas kernels, shards(): pl.pallas_call(write_kernel, out_shape=(layer_shape, emb_shape, jax.Shape...  3.86 us

profile of v3, /device:TPU:0, one launch (start us, length us, event | category | flops | bytes accessed | tf_op | source)
XLA Modules:
  0.0 40.1 jit_solution(3682172655946140975)
XLA Ops:
  0.6 35.6 %interaction_layer.1 = (bf16[8,192,256]{2,1,0:T(8,128)(2,1)}, bf16[32,64,96]{2,1,0:T(8,128)(2,1)}, bf16[48,16,128]{2,1,0:T(8,128)(2,1)}) custom-call(bf16[32,64,192]{2,1,0:T(8,128)(2,1)} %pooled.1, bf16[128,256]{1,0:T(8,128)(2,1)} %lc_w.1, bf16[256,128]{1,0:T(8,128)(2,1)} %proj_w.1, bf16[192,128]{1,0:T(8,128)(2,1)} %bitcast.5, bf16[8,192,256]{2,1,0:T(8,128)(2,1)} %bitcast.4), custom_call_target="tpu_custom_call" | custom-call | tf_op jit(solution)/shard_map/interaction_layer/pallas_call | solution.py:395
  36.2 3.9 %write_outputs.1 = (bf16[8,192,256]{2,1,0:T(8,128)(2,1)}, bf16[32,64,96]{2,1,0:T(8,128)(2,1)}, f32[128,256]{1,0:T(8,128)}, f32[256,128]{1,0:T(8,128)}, f32[192,128]{1,0:T(8,128)}) custom-call(bf16[8,192,256]{2,1,0:T(8,128)(2,1)} %get-tuple-element.13.layer, bf16[32,64,96]{2,1,0:T(8,128)(2,1)} %get-tuple-element.14.emb, ...), custom_call_target="tpu_custom_call" | custom-call | tf_op jit(solution)/shard_map/write_outputs/pallas_call | solution.py:407

commit v4 on v3

--- a/solution.py
+++ b/solution.py
@@ -23,7 +23,7 @@
     kq, jq, dq, cs, pp, fused = cfg["kq"], cfg["jq"], cfg["dq"], cfg["cs"], cfg["pp"], cfg["fused"]
     grads, scratch = (rest[:1], rest[1:]) if fused else (rest[:3], rest[3:])
     (x_ref, gt_ref, g_ref, xt_ref, pw, ww, ow, p_rel, ot_rel, own_ct, own_cgt, own_it, igt, lo, eg, acc_l, acc_p, acc_o,
-     gb, rb1, sb, rb2, fs, loc, x_send, x_recv, w_send, w_recv, e_send, e_recv, r_send, r_recv) = scratch
+     gb, rb1, sb, rb2, fs, loc, x_send, x_recv, w_send, w_recv, f_send, f_recv, c_send, c_recv, e_send, e_recv, r_send, r_recv) = scratch
     chunks = samples // cs
     t = lax.axis_index("table")
     r = lax.axis_index("rep")
@@ -58,16 +58,46 @@
         x_load(c).start()
     pl.semaphore_wait(barrier, signals)
 
-    def x_copy(c, j):
-        to = lax.rem(t + j, tables)
-        return pltpu.make_async_remote_copy(
-            pooled.at[pl.ds(to * samples + c * cs, cs)],
+    chips, rounds = tables // 2, chunks // tensors
+    chip, core = t // 2, lax.rem(t, 2)
+    mate = chip * 2 + lax.rem(core + 1, 2)
+
+    def c_copy(c):
+        return pltpu.make_async_remote_copy(
+            pooled.at[pl.ds(mate * samples + c * cs, cs)],
             x_ref.at[pl.ds(c * cs, cs), t],
-            x_send.at[c, j - 1],
-            x_recv.at[c, j - 1],
-            device_id=peer("table", t, tables, j),
+            c_send.at[c],
+            c_recv.at[c],
+            device_id={"table": mate},
             device_id_type=MESH,
         )
+
+    def x_copy(g, a, b):
+        to = lax.rem(chip + a, chips) * 2 + lax.rem(core + b, 2)
+        first_row = (g * tensors + x) * cs
+        return pltpu.make_async_remote_copy(
+            pooled.at[pl.ds(to * samples + first_row, cs)],
+            x_ref.at[pl.ds(first_row, cs), t],
+            x_send.at[g, a - 1, b],
+            x_recv.at[g, a - 1, b],
+            device_id={"table": to},
+            device_id_type=MESH,
+        )
+
+    def f_copy(g, a, j):
+        source = lax.rem(chip + chips - a, chips) * 2
+        held = x_ref.at[pl.ds((g * tensors + x) * cs, cs), pl.ds(source, 2)]
+        return pltpu.make_async_remote_copy(
+            held, held, f_send.at[g, a - 1, j - 1], f_recv.at[g, a - 1, j - 1],
+            device_id=peer("tensor", x, tensors, j), device_id_type=MESH,
+        )
+
+    def pass_on(g):
+        for a in range(1, chips):
+            for b in range(2):
+                x_copy(g, a, b).wait_recv()
+            for j in range(1, tensors):
+                f_copy(g, a, j).start()
 
     def w_copy(i, j):
         src, dst = w_pairs[i]
@@ -76,9 +106,12 @@
             device_id=peer("tensor", x, tensors, j), device_id_type=MESH,
         )
 
+    for g in range(rounds):
+        for a in range(1, chips):
+            for b in range(2):
+                x_copy(g, a, b).start()
     for c in range(chunks):
-        for j in range(1, tables):
-            x_copy(c, j).start()
+        c_copy(c).start()
     for j in range(1, tensors):
         for i in range(3):
             w_copy(i, j).start()
@@ -101,10 +134,7 @@
 
     lax.fori_loop(0, chunks, before, 0)
 
-    def first(c, carry):
-        x_load(c).wait()
-        for j in range(1, tables):
-            x_copy(c, j).wait_recv()
+    def first(c):
         at = [c * cs + i for i in range(cs)]
         own_rows = [x_ref[s, pl.ds(x * (jq // nr), jq // nr)].reshape(jq, d) for s in at]
         xs = [x_ref[s].reshape(n, d) for s in at]
@@ -129,9 +159,19 @@
             own_ct[s] = comp[i]
             own_cgt[s] = cgrad[i]
             own_it[s] = inter[i]
-        return carry
-
-    lax.fori_loop(0, chunks, first, 0)
+
+    for c in range(chunks):
+        x_load(c).wait()
+        c_copy(c).wait_recv()
+    pass_on(0)
+    for g in range(rounds):
+        first(g * tensors + x)
+        if g + 1 < rounds:
+            pass_on(g + 1)
+        for j in range(1, tensors):
+            for a in range(1, chips):
+                f_copy(g, a, j).wait_recv()
+            first(g * tensors + lax.rem(x + tensors - j, tensors))
 
     part = reps * pp
 
@@ -280,9 +320,15 @@
         for j in range(1, tables):
             e_copy(c, j).wait_recv()
     for c in range(chunks):
+        c_copy(c).wait_send()
         for j in range(1, tables):
-            x_copy(c, j).wait_send()
             e_copy(c, j).wait_send()
+    for g in range(rounds):
+        for a in range(1, chips):
+            for b in range(2):
+                x_copy(g, a, b).wait_send()
+            for j in range(1, tensors):
+                f_copy(g, a, j).wait_send()
     for j in range(1, tensors):
         for i in range(3):
             w_copy(i, j).wait_send()
@@ -295,7 +341,10 @@
             ag_rep(j).wait_send()
 
 
-def write_kernel(layer, emb, pieces, layer_out, emb_out, lc_g, proj_g, out_g, held_l, held_e, sems):
+def write_kernel(layer, emb, pieces, layer_out, emb_out, lc_g, proj_g, out_g,
+                 held_l, held_e, held_g, lc_v, proj_v, out_v, sems):
+    g_load = pltpu.make_async_copy(pieces, held_g, sems.at[0, 8])
+    g_load.start()
     loads, stores = [], []
     for src, held, dst in ((layer, held_l, layer_out), (emb, held_e, emb_out)):
         parts = 4 if src.shape[0] % 4 == 0 else 1
@@ -307,20 +356,24 @@
             stores.append(pltpu.make_async_copy(held.at[rows], dst.at[rows], sems.at[1, at]))
     for load in loads:
         load.start()
-    for load, store in zip(loads, stores):
-        load.wait()
-        store.start()
+    g_load.wait()
     at = 0
     wide = []
     for rows in (lc_g.shape[0], proj_g.shape[1], out_g.shape[1]):
         halves = []
         for _ in range(lc_g.shape[1] // 128):
-            halves.append(pieces[at:at + rows // 16].reshape(rows, 128).astype(F32))
+            halves.append(held_g[at:at + rows // 16].reshape(rows, 128).astype(F32))
             at += rows // 16
         wide.append(halves)
-    lc_g[...] = jnp.concatenate(wide[0], axis=1)
-    proj_g[...] = jnp.concatenate([half.T for half in wide[1]], axis=0)
-    out_g[...] = jnp.concatenate([half.T for half in wide[2]], axis=0)[:out_g.shape[0]]
+    lc_v[...] = jnp.concatenate(wide[0], axis=1)
+    proj_v[...] = jnp.concatenate([half.T for half in wide[1]], axis=0)
+    out_v[...] = jnp.concatenate([half.T for half in wide[2]], axis=0)[:out_g.shape[0]]
+    for i, (held, dst) in enumerate(((lc_v, lc_g), (proj_v, proj_g), (out_v, out_g))):
+        stores.append(pltpu.make_async_copy(held, dst, sems.at[1, 8 + i]))
+        stores[-1].start()
+    for load, store in zip(loads, stores):
+        load.wait()
+        store.start()
     for store in stores:
         store.wait()
 
@@ -331,8 +384,9 @@
     nr = pooled.shape[1]
     jq, kq, dq = lc_weight.shape[0], fm_out.shape[0], d // tensors
     total = samples * reps * tables
-    cs = 2 if samples % 2 == 0 else 1
+    cs = 2 if samples % (2 * tensors) == 0 else 1
     chunks = samples // cs
+    rounds, chips = chunks // tensors, tables // 2
     wide = -(-d // 128) * 128
     pieces = (n // 128) * (jq // 16 + kq // 16) + (wide // 128) * (kq // 16)
     group = tables * reps
@@ -375,10 +429,14 @@
         pltpu.VMEM((max(reps - 1, 1), pp, 16, 128), BF16),
         pltpu.VMEM((held, 16, 128), BF16),
         dma((3 * chunks + 4,)),
-        dma((chunks, peers)),
-        dma((chunks, peers)),
+        dma((rounds, max(chips - 1, 1), 2)),
+        dma((rounds, max(chips - 1, 1), 2)),
         dma((3, wpeers)),
         dma((3, wpeers)),
+        dma((rounds, max(chips - 1, 1), wpeers)),
+        dma((rounds, max(chips - 1, 1), wpeers)),
+        dma((chunks,)),
+        dma((chunks,)),
         dma((chunks, peers)),
         dma((chunks, peers)),
         dma((4, rpeers)),
@@ -413,10 +471,16 @@
                 jax.ShapeDtypeStruct((n, kq), F32),
                 jax.ShapeDtypeStruct((d, kq), F32),
             ),
-            in_specs=[hbm, hbm, vmem],
-            out_specs=(hbm, hbm, vmem, vmem, vmem),
+            in_specs=[hbm] * 3,
+            out_specs=(hbm,) * 5,
             scratch_shapes=[
-                pltpu.VMEM(layer_shape.shape, BF16), pltpu.VMEM(emb_shape.shape, BF16), dma((2, 8)),
+                pltpu.VMEM(layer_shape.shape, BF16),
+                pltpu.VMEM(emb_shape.shape, BF16),
+                pltpu.VMEM(grad_shapes[0].shape, BF16),
+                pltpu.VMEM((jq, n), F32),
+                pltpu.VMEM((n, kq), F32),
+                pltpu.VMEM((d, kq), F32),
+                dma((2, 11)),
             ],
             compiler_params=pltpu.CompilerParams(vmem_limit_bytes=VMEM_BYTES),
             name="write_outputs",

time: 40.3 us -> 38.8 us (0.963)
  Pallas kernels: 39.5 us -> 38 us
    pallas_call x1, Pallas kernels: 3.86 us -> 2.35 us  [shards(): pl.pallas_call(write_kernel, out_shape=(layer_shape, emb_shape, jax.Shape...]
where the time goes in v4:
time: 38.8 us; the launch traced here: 38.6 us
  Pallas kernels  38 us (98%)
  between operations  0.64 us (2%)
    pallas_call x1, Pallas kernels, shards(): pl.pallas_call(functools.partial(layer_kernel, cfg), out_shape=(layer_sha...  35.6 us
    pallas_call x1, Pallas kernels, shards(): pl.pallas_call(write_kernel, out_shape=(layer_shape, emb_shape, jax.Shape...  2.35 us

profile of v4, /device:TPU:0, one launch (start us, length us, event | category | flops | bytes accessed | tf_op | source)
XLA Modules:
  0.0 38.6 jit_solution(14810801040446481559)
XLA Ops:
  0.6 35.6 %interaction_layer.1 = (bf16[8,192,256]{2,1,0:T(8,128)(2,1)}, bf16[32,64,96]{2,1,0:T(8,128)(2,1)}, bf16[48,16,128]{2,1,0:T(8,128)(2,1)}) custom-call(bf16[32,64,192]{2,1,0:T(8,128)(2,1)} %pooled.1, bf16[128,256]{1,0:T(8,128)(2,1)} %lc_w.1, bf16[256,128]{1,0:T(8,128)(2,1)} %proj_w.1, bf16[192,128]{1,0:T(8,128)(2,1)} %bitcast.5, bf16[8,192,256]{2,1,0:T(8,128)(2,1)} %bitcast.4), custom_call_target="tpu_custom_call" | custom-call | tf_op jit(solution)/shard_map/interaction_layer/pallas_call | solution.py:453
  36.3 2.3 %write_outputs.1 = (bf16[8,192,256]{2,1,0:T(8,128)(2,1)}, bf16[32,64,96]{2,1,0:T(8,128)(2,1)}, f32[128,256]{1,0:T(8,128)}, f32[256,128]{1,0:T(8,128)}, f32[192,128]{1,0:T(8,128)}) custom-call(bf16[8,192,256]{2,1,0:T(8,128)(2,1)} %get-tuple-element.13.layer, bf16[32,64,96]{2,1,0:T(8,128)(2,1)} %get-tuple-element.14.emb, ...), custom_call_target="tpu_custom_call" | custom-call | tf_op jit(solution)/shard_map/write_outputs/pallas_call | solution.py:465

commit v5 on v4

--- a/solution.py
+++ b/solution.py
@@ -22,8 +22,8 @@
     samples, nr, n, d = cfg["samples"], cfg["nr"], cfg["n"], cfg["d"]
     kq, jq, dq, cs, pp, fused = cfg["kq"], cfg["jq"], cfg["dq"], cfg["cs"], cfg["pp"], cfg["fused"]
     grads, scratch = (rest[:1], rest[1:]) if fused else (rest[:3], rest[3:])
-    (x_ref, gt_ref, g_ref, xt_ref, pw, ww, ow, p_rel, ot_rel, own_ct, own_cgt, own_it, igt, lo, eg, acc_l, acc_p, acc_o,
-     gb, rb1, sb, rb2, fs, loc, x_send, x_recv, w_send, w_recv, f_send, f_recv, c_send, c_recv, e_send, e_recv, r_send, r_recv) = scratch
+    (x_ref, gt_ref, g_ref, xt_ref, pw, ww, ow, p_rel, ot_rel, own_ct, own_cgt, own_it, igt, lo, eg, er, xin, xout, acc_l, acc_p, acc_o,
+     gb, rb1, sb, rb2, fs, loc, x_send, x_recv, w_send, w_recv, f_send, f_recv, c_send, c_recv, e_out, e_send, e_recv, r_send, r_recv) = scratch
     chunks = samples // cs
     t = lax.axis_index("table")
     r = lax.axis_index("rep")
@@ -40,22 +40,29 @@
             pl.semaphore_signal(barrier, inc=1, device_id=peer(axis, me, size, j), device_id_type=MESH)
             signals += 1
 
-    g_load = pltpu.make_async_copy(cot, gt_ref, loc.at[chunks])
-
-    def x_load(c):
-        return pltpu.make_async_copy(
-            pooled.at[pl.ds(t * samples + c * cs, cs)], x_ref.at[pl.ds(c * cs, cs), t], loc.at[c]
-        )
+    g_load = pltpu.make_async_copy(cot, gt_ref, loc.at[0])
+
+    def x_load(i, to):
+        rows = pl.ds(to * samples, samples)
+        return pltpu.make_async_copy(pooled.at[rows], xin.at[rows], loc.at[4 + 2 * chunks + i])
 
     w_pairs = ((proj_w, pw), (out_w, ow), (lc_w, ww))
     w_loads = [
-        pltpu.make_async_copy(src, dst.at[x], loc.at[chunks + 1 + i]) for i, (src, dst) in enumerate(w_pairs)
+        pltpu.make_async_copy(src, dst.at[x], loc.at[1 + i]) for i, (src, dst) in enumerate(w_pairs)
     ]
+    targets = [lax.rem(t + j, tables) for j in range(tables)]
+    for i, to in enumerate(targets):
+        x_load(i, to).start()
     for load in w_loads:
         load.start()
     g_load.start()
-    for c in range(chunks):
-        x_load(c).start()
+    for i, to in enumerate(targets):
+        rows = pl.ds(to * samples, samples)
+        x_load(i, to).wait()
+        if i == 0:
+            x_ref[:, t, :, :d] = xin[rows]
+        else:
+            xout[rows, :, :d] = xin[rows]
     pl.semaphore_wait(barrier, signals)
 
     chips, rounds = tables // 2, chunks // tensors
@@ -64,7 +71,7 @@
 
     def c_copy(c):
         return pltpu.make_async_remote_copy(
-            pooled.at[pl.ds(mate * samples + c * cs, cs)],
+            xout.at[pl.ds(mate * samples + c * cs, cs)],
             x_ref.at[pl.ds(c * cs, cs), t],
             c_send.at[c],
             c_recv.at[c],
@@ -76,7 +83,7 @@
         to = lax.rem(chip + a, chips) * 2 + lax.rem(core + b, 2)
         first_row = (g * tensors + x) * cs
         return pltpu.make_async_remote_copy(
-            pooled.at[pl.ds(to * samples + first_row, cs)],
+            xout.at[pl.ds(to * samples + first_row, cs)],
             x_ref.at[pl.ds(first_row, cs), t],
             x_send.at[g, a - 1, b],
             x_recv.at[g, a - 1, b],
@@ -136,8 +143,8 @@
 
     def first(c):
         at = [c * cs + i for i in range(cs)]
-        own_rows = [x_ref[s, pl.ds(x * (jq // nr), jq // nr)].reshape(jq, d) for s in at]
-        xs = [x_ref[s].reshape(n, d) for s in at]
+        own_rows = [x_ref[s, pl.ds(x * (jq // nr), jq // nr), :, :d].reshape(jq, d) for s in at]
+        xs = [x_ref[s, :, :, :d].reshape(n, d) for s in at]
         xt = [v.T for v in xs]
         comp = [dot_nn(own_pt, v).astype(BF16) for v in xs]
         cgrad = [dot_nn(igt[s], v).astype(BF16) for s, v in zip(at, xs)]
@@ -161,7 +168,6 @@
             own_it[s] = inter[i]
 
     for c in range(chunks):
-        x_load(c).wait()
         c_copy(c).wait_recv()
     pass_on(0)
     for g in range(rounds):
@@ -256,18 +262,18 @@
 
     def lo_store(c):
         rows = pl.ds(c * cs, cs)
-        return pltpu.make_async_copy(lo.at[rows], layer.at[rows], loc.at[chunks + 4 + c])
+        return pltpu.make_async_copy(lo.at[rows], layer.at[rows], loc.at[4 + c])
 
     def e_store(c):
         return pltpu.make_async_copy(
-            eg.at[pl.ds(c * cs, cs), t], emb.at[pl.ds(t * samples + c * cs, cs)], loc.at[2 * chunks + 4 + c]
+            eg.at[pl.ds(c * cs, cs), t], emb.at[pl.ds(t * samples + c * cs, cs)], loc.at[4 + chunks + c]
         )
 
     def e_copy(c, j):
         to = lax.rem(t + j, tables)
         return pltpu.make_async_remote_copy(
             eg.at[pl.ds(c * cs, cs), to],
-            emb.at[pl.ds(t * samples + c * cs, cs)],
+            er.at[pl.ds(t * samples + c * cs, cs)],
             e_send.at[c, j - 1],
             e_recv.at[c, j - 1],
             device_id=peer("table", t, tables, j),
@@ -276,7 +282,7 @@
 
     def second(c, carry):
         at = [c * cs + i for i in range(cs)]
-        xs = [x_ref[s].reshape(n, d) for s in at]
+        xs = [x_ref[s, :, :, :d].reshape(n, d) for s in at]
         w_all = ww[...].reshape(n, n)
         igrad_t = [[dot_nn(v, gt_ref[s]).astype(BF16) for v in other_o] for s in at]
         comp = [[dot_nn(v, w).astype(BF16) for v in other_pt] for w in xs]
@@ -291,7 +297,7 @@
             own = grad[:, :dq]
             for q in range(1, tensors):
                 own = jnp.where(x == q, grad[:, q * dq:(q + 1) * dq], own)
-            eg[s] = own.reshape(tables, nr, dq).astype(BF16)
+            eg[s, :, :, :dq] = own.reshape(tables, nr, dq).astype(BF16)
         for j in range(1, tables):
             e_copy(c, j).start()
         e_store(c).start()
@@ -306,6 +312,15 @@
 
     lax.fori_loop(0, chunks, second, 0)
 
+    def er_store(c, j):
+        rows = pl.ds(lax.rem(t + tables - j, tables) * samples + c * cs, cs)
+        return pltpu.make_async_copy(er.at[rows], emb.at[rows], e_out.at[c, j - 1])
+
+    for c in range(chunks):
+        for j in range(1, tables):
+            e_copy(c, j).wait_recv()
+            er_store(c, j).start()
+
     if fused:
         for j in range(1, tables):
             ag_table(j).wait_recv()
@@ -318,7 +333,7 @@
         lo_store(c).wait()
         e_store(c).wait()
         for j in range(1, tables):
-            e_copy(c, j).wait_recv()
+            er_store(c, j).wait()
     for c in range(chunks):
         c_copy(c).wait_send()
         for j in range(1, tables):
@@ -342,18 +357,19 @@
 
 
 def write_kernel(layer, emb, pieces, layer_out, emb_out, lc_g, proj_g, out_g,
-                 held_l, held_e, held_g, lc_v, proj_v, out_v, sems):
+                 held_l, held_e, narrow_e, held_g, lc_v, proj_v, out_v, sems):
     g_load = pltpu.make_async_copy(pieces, held_g, sems.at[0, 8])
     g_load.start()
     loads, stores = [], []
-    for src, held, dst in ((layer, held_l, layer_out), (emb, held_e, emb_out)):
+    dq = emb_out.shape[2]
+    for src, held, ready, dst in ((emb, held_e, narrow_e, emb_out), (layer, held_l, held_l, layer_out)):
         parts = 4 if src.shape[0] % 4 == 0 else 1
         size = src.shape[0] // parts
         for p in range(parts):
             rows = pl.ds(p * size, size)
             at = len(loads)
             loads.append(pltpu.make_async_copy(src.at[rows], held.at[rows], sems.at[0, at]))
-            stores.append(pltpu.make_async_copy(held.at[rows], dst.at[rows], sems.at[1, at]))
+            stores.append((rows, ready is held, pltpu.make_async_copy(ready.at[rows], dst.at[rows], sems.at[1, at])))
     for load in loads:
         load.start()
     g_load.wait()
@@ -368,13 +384,18 @@
     lc_v[...] = jnp.concatenate(wide[0], axis=1)
     proj_v[...] = jnp.concatenate([half.T for half in wide[1]], axis=0)
     out_v[...] = jnp.concatenate([half.T for half in wide[2]], axis=0)[:out_g.shape[0]]
-    for i, (held, dst) in enumerate(((lc_v, lc_g), (proj_v, proj_g), (out_v, out_g))):
-        stores.append(pltpu.make_async_copy(held, dst, sems.at[1, 8 + i]))
-        stores[-1].start()
-    for load, store in zip(loads, stores):
+    grads = [
+        pltpu.make_async_copy(held, dst, sems.at[1, 8 + i])
+        for i, (held, dst) in enumerate(((lc_v, lc_g), (proj_v, proj_g), (out_v, out_g)))
+    ]
+    for store in grads:
+        store.start()
+    for load, (rows, whole, store) in zip(loads, stores):
         load.wait()
+        if not whole:
+            narrow_e[rows] = held_e[rows, :, :dq]
         store.start()
-    for store in stores:
+    for store in grads + [store for _, _, store in stores]:
         store.wait()
 
 
@@ -387,7 +408,7 @@
     cs = 2 if samples % (2 * tensors) == 0 else 1
     chunks = samples // cs
     rounds, chips = chunks // tensors, tables // 2
-    wide = -(-d // 128) * 128
+    wide, dq_wide = -(-d // 128) * 128, -(-dq // 128) * 128
     pieces = (n // 128) * (jq // 16 + kq // 16) + (wide // 128) * (kq // 16)
     group = tables * reps
     fused = pieces % group == 0 and wide == n and jq % 16 == 0 and kq % 16 == 0
@@ -405,7 +426,7 @@
     rpeers = max(tables - 1, reps - 1, 1)
     k = kq * tensors
     scratch = [
-        pltpu.VMEM((samples, tables, nr, d), BF16),
+        pltpu.VMEM((samples, tables, nr, wide), BF16),
         pltpu.VMEM((samples, d, n), BF16),
         pltpu.VMEM((samples, n, d), BF16),
         pltpu.VMEM((samples, d, n), BF16),
@@ -419,7 +440,10 @@
         pltpu.VMEM((samples, kq, n), BF16),
         pltpu.VMEM((samples, kq, n), BF16),
         pltpu.VMEM((samples, d, n), BF16),
-        pltpu.VMEM((samples, tables, nr, dq), BF16),
+        pltpu.VMEM((samples, tables, nr, dq_wide), BF16),
+        pltpu.VMEM((tables * samples, nr, dq_wide), BF16),
+        pltpu.VMEM((tables * samples, nr, d), BF16),
+        pltpu.VMEM((tables * samples, nr, wide), BF16),
         pltpu.VMEM((jq, n), F32),
         pltpu.VMEM((kq, n), F32),
         pltpu.VMEM((kq, wide), F32),
@@ -428,7 +452,7 @@
         pltpu.VMEM((part, 16, 128), BF16),
         pltpu.VMEM((max(reps - 1, 1), pp, 16, 128), BF16),
         pltpu.VMEM((held, 16, 128), BF16),
-        dma((3 * chunks + 4,)),
+        dma((2 * chunks + 4 + tables,)),
         dma((rounds, max(chips - 1, 1), 2)),
         dma((rounds, max(chips - 1, 1), 2)),
         dma((3, wpeers)),
@@ -439,6 +463,7 @@
         dma((chunks,)),
         dma((chunks, peers)),
         dma((chunks, peers)),
+        dma((chunks, peers)),
         dma((4, rpeers)),
         dma((4, rpeers)),
     ]
@@ -446,13 +471,14 @@
     vmem = pl.BlockSpec(memory_space=pltpu.VMEM)
     layer_shape = jax.ShapeDtypeStruct((samples, d, n), BF16)
     emb_shape = jax.ShapeDtypeStruct((pooled.shape[0], nr, dq), BF16)
+    emb_wide = jax.ShapeDtypeStruct((pooled.shape[0], nr, dq_wide), BF16)
     if fused:
         grad_shapes = (jax.ShapeDtypeStruct((pieces, 16, 128), BF16),)
     else:
         grad_shapes = tuple(jax.ShapeDtypeStruct(s, F32) for s in ((jq, n), (kq, n), (kq, d)))
     layer, emb, *grads = pl.pallas_call(
         functools.partial(layer_kernel, cfg),
-        out_shape=(layer_shape, emb_shape, *grad_shapes),
+        out_shape=(layer_shape, emb_wide, *grad_shapes),
         in_specs=[hbm] * 5,
         out_specs=(hbm, hbm) + (vmem,) * len(grad_shapes),
         scratch_shapes=scratch,
@@ -475,6 +501,7 @@
             out_specs=(hbm,) * 5,
             scratch_shapes=[
                 pltpu.VMEM(layer_shape.shape, BF16),
+                pltpu.VMEM(emb_wide.shape, BF16),
                 pltpu.VMEM(emb_shape.shape, BF16),
                 pltpu.VMEM(grad_shapes[0].shape, BF16),
                 pltpu.VMEM((jq, n), F32),
@@ -489,6 +516,7 @@
     else:
         lc_g, proj_t, out_g = lax.psum(tuple(grads), ("rep", "table"))
         proj_g = proj_t.T
+        emb = emb[:, :, :dq]
     return layer.transpose(0, 2, 1), emb, lc_g, proj_g, out_g
 
 

time: 38.8 us -> 39.1 us (level)
  no operation moved by 1% of the time
where the time goes in v5:
time: 39.1 us; the launch traced here: 39 us
  Pallas kernels  38.3 us (98%)
  between operations  0.64 us (2%)
    pallas_call x1, Pallas kernels, shards(): pl.pallas_call(functools.partial(layer_kernel, cfg), out_shape=(layer_sha...  36 us
    pallas_call x1, Pallas kernels, shards(): pl.pallas_call(write_kernel, out_shape=(layer_shape, emb_shape, jax.Shape...  2.34 us

profile of v5, /device:TPU:0, one launch (start us, length us, event | category | flops | bytes accessed | tf_op | source)
XLA Modules:
  0.0 39.0 jit_solution(11491513485665107755)
XLA Ops:
  0.6 36.0 %interaction_layer.1 = (bf16[8,192,256]{2,1,0:T(8,128)(2,1)}, bf16[32,64,128]{2,1,0:T(8,128)(2,1)}, bf16[48,16,128]{2,1,0:T(8,128)(2,1)}) custom-call(bf16[32,64,192]{2,1,0:T(8,128)(2,1)} %pooled.1, bf16[128,256]{1,0:T(8,128)(2,1)} %lc_w.1, bf16[256,128]{1,0:T(8,128)(2,1)} %proj_w.1, bf16[192,128]{1,0:T(8,128)(2,1)} %bitcast.5, bf16[8,192,256]{2,1,0:T(8,128)(2,1)} %bitcast.4), custom_call_target="tpu_custom_call" | custom-call | tf_op jit(solution)/shard_map/interaction_layer/pallas_call | solution.py:479
  36.6 2.3 %write_outputs.1 = (bf16[8,192,256]{2,1,0:T(8,128)(2,1)}, bf16[32,64,96]{2,1,0:T(8,128)(2,1)}, f32[128,256]{1,0:T(8,128)}, f32[256,128]{1,0:T(8,128)}, f32[192,128]{1,0:T(8,128)}) custom-call(bf16[8,192,256]{2,1,0:T(8,128)(2,1)} %get-tuple-element.13.layer, bf16[32,64,128]{2,1,0:T(8,128)(2,1)} %get-tuple-element.14.emb, ...), custom_call_target="tpu_custom_call" | custom-call | tf_op jit(solution)/shard_map/write_outputs/pallas_call | solution.py:491

commit v6 on v4

--- a/solution.py
+++ b/solution.py
@@ -17,14 +17,18 @@
     return jnp.dot(a, b, preferred_element_type=F32)
 
 
+def dot_nt(a, b):
+    return lax.dot_general(a, b, (((1,), (1,)), ((), ())), preferred_element_type=F32)
+
+
 def layer_kernel(cfg, pooled, lc_w, proj_w, out_w, cot, layer, emb, *rest):
     tables, reps, tensors = cfg["tables"], cfg["reps"], cfg["tensors"]
     samples, nr, n, d = cfg["samples"], cfg["nr"], cfg["n"], cfg["d"]
     kq, jq, dq, cs, pp, fused = cfg["kq"], cfg["jq"], cfg["dq"], cfg["cs"], cfg["pp"], cfg["fused"]
     grads, scratch = (rest[:1], rest[1:]) if fused else (rest[:3], rest[3:])
-    (x_ref, gt_ref, g_ref, xt_ref, pw, ww, ow, p_rel, ot_rel, own_ct, own_cgt, own_it, igt, lo, eg, acc_l, acc_p, acc_o,
+    (x_ref, gt_ref, g_ref, pw, ww, ow, p_rel, ot_rel, o_rel, w_t, back, c_ref, cg_ref, i_ref, ig_ref, lo, eg, acc_l, acc_p, acc_o,
      gb, rb1, sb, rb2, fs, loc, x_send, x_recv, w_send, w_recv, f_send, f_recv, c_send, c_recv, e_send, e_recv, r_send, r_recv) = scratch
-    chunks = samples // cs
+    chunks, k = samples // cs, tensors * kq
     t = lax.axis_index("table")
     r = lax.axis_index("rep")
     x = lax.axis_index("tensor")
@@ -106,30 +110,37 @@
             device_id=peer("tensor", x, tensors, j), device_id_type=MESH,
         )
 
+    for j in range(1, tensors):
+        for i in range(3):
+            w_copy(i, j).start()
     for g in range(rounds):
         for a in range(1, chips):
             for b in range(2):
                 x_copy(g, a, b).start()
     for c in range(chunks):
         c_copy(c).start()
-    for j in range(1, tensors):
-        for i in range(3):
-            w_copy(i, j).start()
-
-    for load in w_loads:
-        load.wait()
-    own_pt, own_o = pw[x].T, ow[x].T
+
     acc_l[...] = jnp.zeros_like(acc_l)
     acc_p[...] = jnp.zeros_like(acc_p)
     acc_o[...] = jnp.zeros_like(acc_o)
     g_load.wait()
+    for s in range(samples):
+        g_ref[s] = gt_ref[s].T
+    for load in w_loads:
+        load.wait()
+    for j in range(1, tensors):
+        for i in range(2):
+            w_copy(i, j).wait_recv()
+    order = [x] + [lax.rem(x + j, tensors) for j in range(1, tensors)]
+    p_rel[...] = jnp.concatenate([pw[q] for q in order], axis=1)
+    ot_rel[...] = jnp.concatenate([ow[q] for q in order], axis=1)
+    o_rel[...] = ot_rel[...].T
+    back[:k] = p_rel[...].T
 
     def before(c, carry):
-        at = [c * cs + i for i in range(cs)]
-        for s in at:
-            gt = gt_ref[s]
-            g_ref[s] = gt.T
-            igt[s] = dot_nn(own_o, gt).astype(BF16)
+        rows = pl.ds(c * cs, cs)
+        igrad = dot_nn(g_ref[rows].reshape(cs * n, d), ot_rel[...])
+        ig_ref[rows] = igrad.astype(BF16).reshape(cs, n, k)
         return carry
 
     lax.fori_loop(0, chunks, before, 0)
@@ -139,26 +150,26 @@
         own_rows = [x_ref[s, pl.ds(x * (jq // nr), jq // nr)].reshape(jq, d) for s in at]
         xs = [x_ref[s].reshape(n, d) for s in at]
         xt = [v.T for v in xs]
-        comp = [dot_nn(own_pt, v).astype(BF16) for v in xs]
-        cgrad = [dot_nn(igt[s], v).astype(BF16) for s, v in zip(at, xs)]
+        comp = dot_nn(jnp.concatenate(xt, axis=0), p_rel[...]).astype(BF16)
+        comp = [comp[i * d:(i + 1) * d] for i in range(cs)]
+        cgrad = [dot_nn(v, ig_ref[s]).astype(BF16) for s, v in zip(at, xt)]
         sum_l = acc_l[...]
         for s, v in zip(at, own_rows):
             sum_l = sum_l + dot_nn(v, gt_ref[s])
-        inter = [dot_nn(v, w).astype(BF16) for v, w in zip(comp, xt)]
+        inter = [dot_nn(v, w).astype(BF16) for v, w in zip(xs, comp)]
         sum_p = acc_p[...]
-        for v, w in zip(cgrad, xt):
-            sum_p = sum_p + dot_nn(v, w)
-        sum_o = acc_o[:, :d]
+        for v, w in zip(xs, cgrad):
+            sum_p = sum_p + dot_nn(v, w[:, :kq])
+        sum_o = acc_o[:d]
         for s, v in zip(at, inter):
-            sum_o = sum_o + dot_nn(v, g_ref[s])
+            sum_o = sum_o + dot_nn(gt_ref[s], v[:, :kq])
         acc_l[...] = sum_l
         acc_p[...] = sum_p
-        acc_o[:, :d] = sum_o
+        acc_o[:d] = sum_o
         for i, s in enumerate(at):
-            xt_ref[s] = xt[i]
-            own_ct[s] = comp[i]
-            own_cgt[s] = cgrad[i]
-            own_it[s] = inter[i]
+            c_ref[s] = comp[i]
+            cg_ref[s] = cgrad[i]
+            i_ref[s] = inter[i]
 
     for c in range(chunks):
         x_load(c).wait()
@@ -203,11 +214,12 @@
             device_id=peer("table", t, tables, j), device_id_type=MESH,
         )
 
-    layout = ((acc_l, jq, cfg["wide_scale"]), (acc_p, kq, cfg["wide_scale"]), (acc_o, kq, cfg["out_scale"]))
+    layout = ((acc_l, cfg["wide_scale"]), (acc_p, cfg["wide_scale"]), (acc_o, cfg["out_scale"]))
     if fused:
         at = 0
-        for ref, rows, scale in layout:
-            for h in range(n // 128):
+        for ref, scale in layout:
+            rows = ref.shape[0]
+            for h in range(ref.shape[1] // 128):
                 value = (ref[:, h * 128:(h + 1) * 128] * scale).astype(BF16)
                 gb[at:at + rows // 16] = value.reshape(rows // 16, 16, 128)
                 at += rows // 16
@@ -246,13 +258,10 @@
                 ag_table(j).start()
 
     for j in range(1, tensors):
-        for i in range(3):
-            w_copy(i, j).wait_recv()
-    order = [x] + [lax.rem(x + j, tensors) for j in range(1, tensors)]
-    p_rel[...] = jnp.concatenate([pw[q] for q in order], axis=1)
-    ot_rel[...] = jnp.concatenate([ow[q] for q in order], axis=1)
-    other_pt = [pw[q].T for q in order[1:]]
-    other_o = [ow[q].T for q in order[1:]]
+        w_copy(2, j).wait_recv()
+    w_t[...] = ww[...].reshape(n, n).T
+    back[k:] = w_t[...]
+    own_d = pl.ds(pl.multiple_of(x * dq, dq), dq)
 
     def lo_store(c):
         rows = pl.ds(c * cs, cs)
@@ -276,30 +285,23 @@
 
     def second(c, carry):
         at = [c * cs + i for i in range(cs)]
-        xs = [x_ref[s].reshape(n, d) for s in at]
-        w_all = ww[...].reshape(n, n)
-        igrad_t = [[dot_nn(v, gt_ref[s]).astype(BF16) for v in other_o] for s in at]
-        comp = [[dot_nn(v, w).astype(BF16) for v in other_pt] for w in xs]
-        igrad = [dot_nn(g_ref[s], ot_rel[...]).astype(BF16) for s in at]
-        cgrad = [[dot_nn(v, w).astype(BF16) for v in vs] for vs, w in zip(igrad_t, xs)]
-        inter = [[dot_nn(v, xt_ref[s]).astype(BF16) for v in vs] for vs, s in zip(comp, at)]
+        rows = pl.ds(c * cs, cs)
+        gt = gt_ref[rows, own_d]
+        left = jnp.concatenate([cg_ref[rows, own_d].reshape(cs * dq, k), gt.reshape(cs * dq, n)], axis=1)
+        shared = dot_nn(left, back[...]) + gt.astype(F32).reshape(cs * dq, n)
+        terms = [dot_nt(c_ref[s, own_d], ig_ref[s]) for s in at]
         for i, s in enumerate(at):
-            gs = g_ref[s]
-            left = jnp.concatenate([igrad[i], p_rel[...], w_all], axis=1)
-            right = jnp.concatenate([own_ct[s], *comp[i], own_cgt[s], *cgrad[i], gs], axis=0)
-            grad = dot_nn(left, right) + gs.astype(F32)
-            own = grad[:, :dq]
-            for q in range(1, tensors):
-                own = jnp.where(x == q, grad[:, q * dq:(q + 1) * dq], own)
-            eg[s] = own.reshape(tables, nr, dq).astype(BF16)
+            grad = shared[i * dq:(i + 1) * dq] + terms[i]
+            eg[s] = grad.T.reshape(tables, nr, dq).astype(BF16)
         for j in range(1, tables):
             e_copy(c, j).start()
         e_store(c).start()
+        mixture = dot_nn(i_ref[rows].reshape(cs * n, k), o_rel[...])
+        xs = [x_ref[s].reshape(n, d) for s in at]
+        mixed = [dot_nn(w_t[...], v) for v in xs]
         for i, s in enumerate(at):
-            xt = xt_ref[s]
-            left = jnp.concatenate([ot_rel[...], xt], axis=1)
-            right = jnp.concatenate([own_it[s], *inter[i], w_all], axis=0)
-            lo[s] = (dot_nn(left, right) + xt.astype(F32)).astype(BF16)
+            out = xs[i].astype(F32) + (mixture[i * n:(i + 1) * n] + mixed[i])
+            lo[s] = out.astype(BF16).T
         lo_store(c).start()
         reduce_step(c)
         return carry
@@ -311,8 +313,8 @@
             ag_table(j).wait_recv()
         grads[0][...] = fs[...]
     else:
-        for ref, (acc, rows, scale) in zip(grads, layout):
-            ref[...] = acc[:, :ref.shape[1]] * scale
+        for ref, (acc, scale) in zip(grads, layout):
+            ref[...] = acc[:ref.shape[0]] * scale
 
     for c in range(chunks):
         lo_store(c).wait()
@@ -358,16 +360,11 @@
         load.start()
     g_load.wait()
     at = 0
-    wide = []
-    for rows in (lc_g.shape[0], proj_g.shape[1], out_g.shape[1]):
-        halves = []
-        for _ in range(lc_g.shape[1] // 128):
-            halves.append(held_g[at:at + rows // 16].reshape(rows, 128).astype(F32))
-            at += rows // 16
-        wide.append(halves)
-    lc_v[...] = jnp.concatenate(wide[0], axis=1)
-    proj_v[...] = jnp.concatenate([half.T for half in wide[1]], axis=0)
-    out_v[...] = jnp.concatenate([half.T for half in wide[2]], axis=0)[:out_g.shape[0]]
+    for ref, rows in ((lc_v, lc_v.shape[0]), (proj_v, proj_v.shape[0]), (out_v, out_v.shape[0])):
+        padded = -(-rows // 128) * 128
+        for h in range(ref.shape[1] // 128):
+            ref[:, h * 128:(h + 1) * 128] = held_g[at:at + rows // 16].reshape(rows, 128).astype(F32)
+            at += padded // 16
     for i, (held, dst) in enumerate(((lc_v, lc_g), (proj_v, proj_g), (out_v, out_g))):
         stores.append(pltpu.make_async_copy(held, dst, sems.at[1, 8 + i]))
         stores[-1].start()
@@ -388,9 +385,9 @@
     chunks = samples // cs
     rounds, chips = chunks // tensors, tables // 2
     wide = -(-d // 128) * 128
-    pieces = (n // 128) * (jq // 16 + kq // 16) + (wide // 128) * (kq // 16)
+    pieces = (n // 128) * (jq // 16) + (kq // 128) * (n // 16 + wide // 16)
     group = tables * reps
-    fused = pieces % group == 0 and wide == n and jq % 16 == 0 and kq % 16 == 0
+    fused = pieces % group == 0 and n % 128 == 0 and jq % 128 == 0 and kq % 128 == 0
     pp = pieces // group if fused else 1
     cfg = dict(
         tables=tables, reps=reps, tensors=tensors, samples=samples, nr=nr, n=n, d=d, kq=kq, jq=jq, dq=dq,
@@ -408,21 +405,23 @@
         pltpu.VMEM((samples, tables, nr, d), BF16),
         pltpu.VMEM((samples, d, n), BF16),
         pltpu.VMEM((samples, n, d), BF16),
-        pltpu.VMEM((samples, d, n), BF16),
         pltpu.VMEM((tensors, n, kq), BF16),
         pltpu.VMEM((tensors, jq, n), BF16),
         pltpu.VMEM((tensors, d, kq), BF16),
         pltpu.VMEM((n, k), BF16),
         pltpu.VMEM((d, k), BF16),
-        pltpu.VMEM((samples, kq, d), BF16),
-        pltpu.VMEM((samples, kq, d), BF16),
-        pltpu.VMEM((samples, kq, n), BF16),
-        pltpu.VMEM((samples, kq, n), BF16),
+        pltpu.VMEM((k, d), BF16),
+        pltpu.VMEM((n, n), BF16),
+        pltpu.VMEM((k + n, n), BF16),
+        pltpu.VMEM((samples, d, k), BF16),
+        pltpu.VMEM((samples, d, k), BF16),
+        pltpu.VMEM((samples, n, k), BF16),
+        pltpu.VMEM((samples, n, k), BF16),
         pltpu.VMEM((samples, d, n), BF16),
         pltpu.VMEM((samples, tables, nr, dq), BF16),
         pltpu.VMEM((jq, n), F32),
-        pltpu.VMEM((kq, n), F32),
-        pltpu.VMEM((kq, wide), F32),
+        pltpu.VMEM((n, kq), F32),
+        pltpu.VMEM((wide, kq), F32),
         pltpu.VMEM((held, 16, 128), BF16),
         pltpu.VMEM((peers, part, 16, 128), BF16),
         pltpu.VMEM((part, 16, 128), BF16),
@@ -449,7 +448,7 @@
     if fused:
         grad_shapes = (jax.ShapeDtypeStruct((pieces, 16, 128), BF16),)
     else:
-        grad_shapes = tuple(jax.ShapeDtypeStruct(s, F32) for s in ((jq, n), (kq, n), (kq, d)))
+        grad_shapes = tuple(jax.ShapeDtypeStruct(s, F32) for s in ((jq, n), (n, kq), (d, kq)))
     layer, emb, *grads = pl.pallas_call(
         functools.partial(layer_kernel, cfg),
         out_shape=(layer_shape, emb_shape, *grad_shapes),
@@ -485,11 +484,9 @@
             compiler_params=pltpu.CompilerParams(vmem_limit_bytes=VMEM_BYTES),
             name="write_outputs",
         )(layer, emb, *grads)
-        out_g = out_t.T
     else:
-        lc_g, proj_t, out_g = lax.psum(tuple(grads), ("rep", "table"))
-        proj_g = proj_t.T
-    return layer.transpose(0, 2, 1), emb, lc_g, proj_g, out_g
+        lc_g, proj_g, out_t = lax.psum(tuple(grads), ("rep", "table"))
+    return layer.transpose(0, 2, 1), emb, lc_g, proj_g, out_t.T
 
 
 def solution(mesh):

time: 38.8 us -> 39.8 us (1.026)
  Pallas kernels: 38 us -> 39 us
    pallas_call x1, Pallas kernels: 35.6 us -> 36.7 us  [shards(): pl.pallas_call(functools.partial(layer_kernel, cfg), out_shape=(layer_sha...]
where the time goes in v6:
time: 39.8 us; the launch traced here: 39.6 us
  Pallas kernels  39 us (98%)
  between operations  0.64 us (2%)
    pallas_call x1, Pallas kernels, shards(): pl.pallas_call(functools.partial(layer_kernel, cfg), out_shape=(layer_sha...  36.7 us
    pallas_call x1, Pallas kernels, shards(): pl.pallas_call(write_kernel, out_shape=(layer_shape, emb_shape, jax.Shape...  2.33 us

profile of v6, /device:TPU:0, one launch (start us, length us, event | category | flops | bytes accessed | tf_op | source)
XLA Modules:
  0.0 39.6 jit_solution(17917490195718951913)
XLA Ops:
  0.6 36.7 %interaction_layer.1 = (bf16[8,192,256]{2,1,0:T(8,128)(2,1)}, bf16[32,64,96]{2,1,0:T(8,128)(2,1)}, bf16[48,16,128]{2,1,0:T(8,128)(2,1)}) custom-call(bf16[32,64,192]{2,1,0:T(8,128)(2,1)} %pooled.1, bf16[128,256]{1,0:T(8,128)(2,1)} %lc_w.1, bf16[256,128]{1,0:T(8,128)(2,1)} %proj_w.1, bf16[192,128]{1,0:T(8,128)(2,1)} %bitcast.5, bf16[8,192,256]{2,1,0:T(8,128)(2,1)} %bitcast.4), custom_call_target="tpu_custom_call" | custom-call | tf_op jit(solution)/shard_map/interaction_layer/pallas_call | solution.py:452
  37.3 2.3 %write_outputs.1 = (bf16[8,192,256]{2,1,0:T(8,128)(2,1)}, bf16[32,64,96]{2,1,0:T(8,128)(2,1)}, f32[128,256]{1,0:T(8,128)}, f32[256,128]{1,0:T(8,128)}, f32[192,128]{1,0:T(8,128)}) custom-call(bf16[8,192,256]{2,1,0:T(8,128)(2,1)} %get-tuple-element.13.layer, bf16[32,64,96]{2,1,0:T(8,128)(2,1)} %get-tuple-element.14.emb, ...), custom_call_target="tpu_custom_call" | custom-call | tf_op jit(solution)/shard_map/write_outputs/pallas_call | solution.py:464

commit v7 on v6

--- a/solution.py
+++ b/solution.py
@@ -44,37 +44,28 @@
             pl.semaphore_signal(barrier, inc=1, device_id=peer(axis, me, size, j), device_id_type=MESH)
             signals += 1
 
-    g_load = pltpu.make_async_copy(cot, gt_ref, loc.at[chunks])
-
-    def x_load(c):
-        return pltpu.make_async_copy(
-            pooled.at[pl.ds(t * samples + c * cs, cs)], x_ref.at[pl.ds(c * cs, cs), t], loc.at[c]
-        )
+    g_load = pltpu.make_async_copy(cot, gt_ref, loc.at[4])
+
+    x_load = pltpu.make_async_copy(pooled.at[pl.ds(t * samples, samples)], x_ref.at[:, t], loc.at[0])
 
     w_pairs = ((proj_w, pw), (out_w, ow), (lc_w, ww))
     w_loads = [
-        pltpu.make_async_copy(src, dst.at[x], loc.at[chunks + 1 + i]) for i, (src, dst) in enumerate(w_pairs)
+        pltpu.make_async_copy(src, dst.at[x], loc.at[1 + i]) for i, (src, dst) in enumerate(w_pairs)
     ]
     for load in w_loads:
         load.start()
     g_load.start()
-    for c in range(chunks):
-        x_load(c).start()
+    x_load.start()
     pl.semaphore_wait(barrier, signals)
 
     chips, rounds = tables // 2, chunks // tensors
     chip, core = t // 2, lax.rem(t, 2)
     mate = chip * 2 + lax.rem(core + 1, 2)
 
-    def c_copy(c):
-        return pltpu.make_async_remote_copy(
-            pooled.at[pl.ds(mate * samples + c * cs, cs)],
-            x_ref.at[pl.ds(c * cs, cs), t],
-            c_send.at[c],
-            c_recv.at[c],
-            device_id={"table": mate},
-            device_id_type=MESH,
-        )
+    c_copy = pltpu.make_async_remote_copy(
+        pooled.at[pl.ds(mate * samples, samples)], x_ref.at[:, t], c_send, c_recv,
+        device_id={"table": mate}, device_id_type=MESH,
+    )
 
     def x_copy(g, a, b):
         to = lax.rem(chip + a, chips) * 2 + lax.rem(core + b, 2)
@@ -117,8 +108,7 @@
         for a in range(1, chips):
             for b in range(2):
                 x_copy(g, a, b).start()
-    for c in range(chunks):
-        c_copy(c).start()
+    c_copy.start()
 
     acc_l[...] = jnp.zeros_like(acc_l)
     acc_p[...] = jnp.zeros_like(acc_p)
@@ -171,9 +161,8 @@
             cg_ref[s] = cgrad[i]
             i_ref[s] = inter[i]
 
-    for c in range(chunks):
-        x_load(c).wait()
-        c_copy(c).wait_recv()
+    x_load.wait()
+    c_copy.wait_recv()
     pass_on(0)
     for g in range(rounds):
         first(g * tensors + x)
@@ -230,8 +219,7 @@
         if not fused:
             return
 
-        @pl.when(c == 0)
-        def _():
+        if c == 0:
             total = gb[pl.ds(t * part, part)].astype(F32)
             for j in range(1, tables):
                 rs_table(j).wait_recv()
@@ -240,8 +228,7 @@
             for j in range(1, reps):
                 rs_rep(j).start()
 
-        @pl.when(c == 1)
-        def _():
+        if c == 1:
             total = sb[pl.ds(r * pp, pp)].astype(F32)
             for j in range(1, reps):
                 rs_rep(j).wait_recv()
@@ -250,8 +237,7 @@
             for j in range(1, reps):
                 ag_rep(j).start()
 
-        @pl.when(c == 2)
-        def _():
+        if c == 2:
             for j in range(1, reps):
                 ag_rep(j).wait_recv()
             for j in range(1, tables):
@@ -265,11 +251,11 @@
 
     def lo_store(c):
         rows = pl.ds(c * cs, cs)
-        return pltpu.make_async_copy(lo.at[rows], layer.at[rows], loc.at[chunks + 4 + c])
+        return pltpu.make_async_copy(lo.at[rows], layer.at[rows], loc.at[5 + c])
 
     def e_store(c):
         return pltpu.make_async_copy(
-            eg.at[pl.ds(c * cs, cs), t], emb.at[pl.ds(t * samples + c * cs, cs)], loc.at[2 * chunks + 4 + c]
+            eg.at[pl.ds(c * cs, cs), t], emb.at[pl.ds(t * samples + c * cs, cs)], loc.at[5 + chunks + c]
         )
 
     def e_copy(c, j):
@@ -283,7 +269,7 @@
             device_id_type=MESH,
         )
 
-    def second(c, carry):
+    def second(c):
         at = [c * cs + i for i in range(cs)]
         rows = pl.ds(c * cs, cs)
         gt = gt_ref[rows, own_d]
@@ -296,6 +282,10 @@
         for j in range(1, tables):
             e_copy(c, j).start()
         e_store(c).start()
+
+    def third(c):
+        at = [c * cs + i for i in range(cs)]
+        rows = pl.ds(c * cs, cs)
         mixture = dot_nn(i_ref[rows].reshape(cs * n, k), o_rel[...])
         xs = [x_ref[s].reshape(n, d) for s in at]
         mixed = [dot_nn(w_t[...], v) for v in xs]
@@ -303,10 +293,11 @@
             out = xs[i].astype(F32) + (mixture[i * n:(i + 1) * n] + mixed[i])
             lo[s] = out.astype(BF16).T
         lo_store(c).start()
-        reduce_step(c)
-        return carry
-
-    lax.fori_loop(0, chunks, second, 0)
+
+    steps = [functools.partial(part, c) for part in (second, third) for c in range(chunks)]
+    for i, step in enumerate(steps):
+        step()
+        reduce_step(i)
 
     if fused:
         for j in range(1, tables):
@@ -322,9 +313,9 @@
         for j in range(1, tables):
             e_copy(c, j).wait_recv()
     for c in range(chunks):
-        c_copy(c).wait_send()
         for j in range(1, tables):
             e_copy(c, j).wait_send()
+    c_copy.wait_send()
     for g in range(rounds):
         for a in range(1, chips):
             for b in range(2):
@@ -381,7 +372,7 @@
     nr = pooled.shape[1]
     jq, kq, dq = lc_weight.shape[0], fm_out.shape[0], d // tensors
     total = samples * reps * tables
-    cs = 2 if samples % (2 * tensors) == 0 else 1
+    cs = max(c for c in (1, 2, 4) if samples % (c * tensors) == 0)
     chunks = samples // cs
     rounds, chips = chunks // tensors, tables // 2
     wide = -(-d // 128) * 128
@@ -427,15 +418,15 @@
         pltpu.VMEM((part, 16, 128), BF16),
         pltpu.VMEM((max(reps - 1, 1), pp, 16, 128), BF16),
         pltpu.VMEM((held, 16, 128), BF16),
-        dma((3 * chunks + 4,)),
+        dma((2 * chunks + 5,)),
         dma((rounds, max(chips - 1, 1), 2)),
         dma((rounds, max(chips - 1, 1), 2)),
         dma((3, wpeers)),
         dma((3, wpeers)),
         dma((rounds, max(chips - 1, 1), wpeers)),
         dma((rounds, max(chips - 1, 1), wpeers)),
-        dma((chunks,)),
-        dma((chunks,)),
+        dma,
+        dma,
         dma((chunks, peers)),
         dma((chunks, peers)),
         dma((4, rpeers)),

time: 39.8 us -> 39.5 us (level)
  no operation moved by 1% of the time
where the time goes in v7:
time: 39.5 us; the launch traced here: 39.4 us
  Pallas kernels  38.8 us (98%)
  between operations  0.64 us (2%)
    pallas_call x1, Pallas kernels, shards(): pl.pallas_call(functools.partial(layer_kernel, cfg), out_shape=(layer_sha...  36.4 us
    pallas_call x1, Pallas kernels, shards(): pl.pallas_call(write_kernel, out_shape=(layer_shape, emb_shape, jax.Shape...  2.33 us

profile of v7, /device:TPU:0, one launch (start us, length us, event | category | flops | bytes accessed | tf_op | source)
XLA Modules:
  0.0 39.4 jit_solution(10149261564490710299)
XLA Ops:
  0.6 36.4 %interaction_layer.1 = (bf16[8,192,256]{2,1,0:T(8,128)(2,1)}, bf16[32,64,96]{2,1,0:T(8,128)(2,1)}, bf16[48,16,128]{2,1,0:T(8,128)(2,1)}) custom-call(bf16[32,64,192]{2,1,0:T(8,128)(2,1)} %pooled.1, bf16[128,256]{1,0:T(8,128)(2,1)} %lc_w.1, bf16[256,128]{1,0:T(8,128)(2,1)} %proj_w.1, bf16[192,128]{1,0:T(8,128)(2,1)} %bitcast.5, bf16[8,192,256]{2,1,0:T(8,128)(2,1)} %bitcast.4), custom_call_target="tpu_custom_call" | custom-call | tf_op jit(solution)/shard_map/interaction_layer/pallas_call | solution.py:443
  37.1 2.3 %write_outputs.1 = (bf16[8,192,256]{2,1,0:T(8,128)(2,1)}, bf16[32,64,96]{2,1,0:T(8,128)(2,1)}, f32[128,256]{1,0:T(8,128)}, f32[256,128]{1,0:T(8,128)}, f32[192,128]{1,0:T(8,128)}) custom-call(bf16[8,192,256]{2,1,0:T(8,128)(2,1)} %get-tuple-element.13.layer, bf16[32,64,96]{2,1,0:T(8,128)(2,1)} %get-tuple-element.14.emb, ...), custom_call_target="tpu_custom_call" | custom-call | tf_op jit(solution)/shard_map/write_outputs/pallas_call | solution.py:455

commit v8 on v4

--- a/solution.py
+++ b/solution.py
@@ -23,7 +23,7 @@
     kq, jq, dq, cs, pp, fused = cfg["kq"], cfg["jq"], cfg["dq"], cfg["cs"], cfg["pp"], cfg["fused"]
     grads, scratch = (rest[:1], rest[1:]) if fused else (rest[:3], rest[3:])
     (x_ref, gt_ref, g_ref, xt_ref, pw, ww, ow, p_rel, ot_rel, own_ct, own_cgt, own_it, igt, lo, eg, acc_l, acc_p, acc_o,
-     gb, rb1, sb, rb2, fs, loc, x_send, x_recv, w_send, w_recv, f_send, f_recv, c_send, c_recv, e_send, e_recv, r_send, r_recv) = scratch
+     gb, rb1, fs, loc, x_send, x_recv, w_send, w_recv, f_send, f_recv, c_send, c_recv, e_send, e_recv, r_send, r_recv) = scratch
     chunks = samples // cs
     t = lax.axis_index("table")
     r = lax.axis_index("rep")
@@ -33,12 +33,19 @@
         return {axis: lax.rem(me + j, size)}
 
     barrier = pltpu.get_barrier_semaphore()
-    groups = [("table", t, tables), ("tensor", x, tensors)] + ([("rep", r, reps)] if fused else [])
-    signals = 0
-    for axis, me, size in groups:
-        for j in range(1, size):
-            pl.semaphore_signal(barrier, inc=1, device_id=peer(axis, me, size, j), device_id_type=MESH)
-            signals += 1
+    group, place = tables * reps, r * tables + t
+
+    def member(j):
+        to = lax.rem(place + j, group)
+        return to, {"rep": to // tables, "table": lax.rem(to, tables)}
+
+    greeted = [peer("tensor", x, tensors, j) for j in range(1, tensors)]
+    if fused:
+        greeted += [member(j)[1] for j in range(1, group)]
+    else:
+        greeted += [peer("table", t, tables, j) for j in range(1, tables)]
+    for device in greeted:
+        pl.semaphore_signal(barrier, inc=1, device_id=device, device_id_type=MESH)
 
     g_load = pltpu.make_async_copy(cot, gt_ref, loc.at[chunks])
 
@@ -56,7 +63,7 @@
     g_load.start()
     for c in range(chunks):
         x_load(c).start()
-    pl.semaphore_wait(barrier, signals)
+    pl.semaphore_wait(barrier, len(greeted))
 
     chips, rounds = tables // 2, chunks // tensors
     chip, core = t // 2, lax.rem(t, 2)
@@ -173,34 +180,18 @@
                 f_copy(g, a, j).wait_recv()
             first(g * tensors + lax.rem(x + tensors - j, tensors))
 
-    part = reps * pp
-
-    def rs_table(j):
-        to = lax.rem(t + j, tables)
-        return pltpu.make_async_remote_copy(
-            gb.at[pl.ds(to * part, part)], rb1.at[j - 1], r_send.at[0, j - 1], r_recv.at[0, j - 1],
-            device_id=peer("table", t, tables, j), device_id_type=MESH,
-        )
-
-    def rs_rep(j):
-        to = lax.rem(r + j, reps)
-        return pltpu.make_async_remote_copy(
-            sb.at[pl.ds(to * pp, pp)], rb2.at[j - 1], r_send.at[1, j - 1], r_recv.at[1, j - 1],
-            device_id=peer("rep", r, reps, j), device_id_type=MESH,
-        )
-
-    def ag_rep(j):
-        mine = fs.at[pl.ds(t * part + r * pp, pp)]
-        return pltpu.make_async_remote_copy(
-            mine, mine, r_send.at[2, j - 1], r_recv.at[2, j - 1],
-            device_id=peer("rep", r, reps, j), device_id_type=MESH,
-        )
-
-    def ag_table(j):
-        mine = fs.at[pl.ds(t * part, part)]
-        return pltpu.make_async_remote_copy(
-            mine, mine, r_send.at[3, j - 1], r_recv.at[3, j - 1],
-            device_id=peer("table", t, tables, j), device_id_type=MESH,
+    def scatter(j):
+        to, device = member(j)
+        return pltpu.make_async_remote_copy(
+            gb.at[pl.ds(to * pp, pp)], rb1.at[j - 1], r_send.at[0, j - 1], r_recv.at[0, j - 1],
+            device_id=device, device_id_type=MESH,
+        )
+
+    def gather(j):
+        mine = fs.at[pl.ds(place * pp, pp)]
+        return pltpu.make_async_remote_copy(
+            mine, mine, r_send.at[1, j - 1], r_recv.at[1, j - 1],
+            device_id=member(j)[1], device_id_type=MESH,
         )
 
     layout = ((acc_l, jq, cfg["wide_scale"]), (acc_p, kq, cfg["wide_scale"]), (acc_o, kq, cfg["out_scale"]))
@@ -211,39 +202,22 @@
                 value = (ref[:, h * 128:(h + 1) * 128] * scale).astype(BF16)
                 gb[at:at + rows // 16] = value.reshape(rows // 16, 16, 128)
                 at += rows // 16
-        for j in range(1, tables):
-            rs_table(j).start()
+        for j in range(1, group):
+            scatter(j).start()
 
     def reduce_step(c):
         if not fused:
             return
 
-        @pl.when(c == 0)
-        def _():
-            total = gb[pl.ds(t * part, part)].astype(F32)
-            for j in range(1, tables):
-                rs_table(j).wait_recv()
-                total = total + rb1[j - 1].astype(F32)
-            sb[...] = total.astype(BF16)
-            for j in range(1, reps):
-                rs_rep(j).start()
-
         @pl.when(c == 1)
         def _():
-            total = sb[pl.ds(r * pp, pp)].astype(F32)
-            for j in range(1, reps):
-                rs_rep(j).wait_recv()
-                total = total + rb2[j - 1].astype(F32)
-            fs[pl.ds(t * part + r * pp, pp)] = total.astype(BF16)
-            for j in range(1, reps):
-                ag_rep(j).start()
-
-        @pl.when(c == 2)
-        def _():
-            for j in range(1, reps):
-                ag_rep(j).wait_recv()
-            for j in range(1, tables):
-                ag_table(j).start()
+            total = gb[pl.ds(place * pp, pp)].astype(F32)
+            for j in range(1, group):
+                scatter(j).wait_recv()
+                total = total + rb1[j - 1].astype(F32)
+            fs[pl.ds(place * pp, pp)] = total.astype(BF16)
+            for j in range(1, group):
+                gather(j).start()
 
     for j in range(1, tensors):
         for i in range(3):
@@ -307,8 +281,8 @@
     lax.fori_loop(0, chunks, second, 0)
 
     if fused:
-        for j in range(1, tables):
-            ag_table(j).wait_recv()
+        for j in range(1, group):
+            gather(j).wait_recv()
         grads[0][...] = fs[...]
     else:
         for ref, (acc, rows, scale) in zip(grads, layout):
@@ -333,12 +307,9 @@
         for i in range(3):
             w_copy(i, j).wait_send()
     if fused:
-        for j in range(1, tables):
-            rs_table(j).wait_send()
-            ag_table(j).wait_send()
-        for j in range(1, reps):
-            rs_rep(j).wait_send()
-            ag_rep(j).wait_send()
+        for j in range(1, group):
+            scatter(j).wait_send()
+            gather(j).wait_send()
 
 
 def write_kernel(layer, emb, pieces, layer_out, emb_out, lc_g, proj_g, out_g,
@@ -397,12 +368,11 @@
         cs=cs, pp=pp, fused=fused,
         wide_scale=float(total * d) ** (-0.5), out_scale=float(total * n * d) ** (-0.5),
     )
-    part = reps * pp if fused else 1
     held = pieces if fused else 1
     dma = pltpu.SemaphoreType.DMA
     peers = max(tables - 1, 1)
     wpeers = max(tensors - 1, 1)
-    rpeers = max(tables - 1, reps - 1, 1)
+    rpeers = max(group - 1, 1) if fused else 1
     k = kq * tensors
     scratch = [
         pltpu.VMEM((samples, tables, nr, d), BF16),
@@ -424,9 +394,7 @@
         pltpu.VMEM((kq, n), F32),
         pltpu.VMEM((kq, wide), F32),
         pltpu.VMEM((held, 16, 128), BF16),
-        pltpu.VMEM((peers, part, 16, 128), BF16),
-        pltpu.VMEM((part, 16, 128), BF16),
-        pltpu.VMEM((max(reps - 1, 1), pp, 16, 128), BF16),
+        pltpu.VMEM((rpeers, pp, 16, 128), BF16),
         pltpu.VMEM((held, 16, 128), BF16),
         dma((3 * chunks + 4,)),
         dma((rounds, max(chips - 1, 1), 2)),
@@ -439,8 +407,8 @@
         dma((chunks,)),
         dma((chunks, peers)),
         dma((chunks, peers)),
-        dma((4, rpeers)),
-        dma((4, rpeers)),
+        dma((2, rpeers)),
+        dma((2, rpeers)),
     ]
     hbm = pl.BlockSpec(memory_space=pl.ANY)
     vmem = pl.BlockSpec(memory_space=pltpu.VMEM)

time: 38.8 us -> 36.5 us (0.941)
  Pallas kernels: 38 us -> 35.7 us
    pallas_call x1, Pallas kernels: 35.6 us -> 33.4 us  [shards(): pl.pallas_call(functools.partial(layer_kernel, cfg), out_shape=(layer_sha...]
where the time goes in v8:
time: 36.5 us; the launch traced here: 36.4 us
  Pallas kernels  35.7 us (98%)
  between operations  0.64 us (2%)
    pallas_call x1, Pallas kernels, shards(): pl.pallas_call(functools.partial(layer_kernel, cfg), out_shape=(layer_sha...  33.4 us
    pallas_call x1, Pallas kernels, shards(): pl.pallas_call(write_kernel, out_shape=(layer_shape, emb_shape, jax.Shape...  2.35 us

profile of v8, /device:TPU:0, one launch (start us, length us, event | category | flops | bytes accessed | tf_op | source)
XLA Modules:
  0.0 36.4 jit_solution(2026611856803820718)
XLA Ops:
  0.6 33.4 %interaction_layer.1 = (bf16[8,192,256]{2,1,0:T(8,128)(2,1)}, bf16[32,64,96]{2,1,0:T(8,128)(2,1)}, bf16[48,16,128]{2,1,0:T(8,128)(2,1)}) custom-call(bf16[32,64,192]{2,1,0:T(8,128)(2,1)} %pooled.1, bf16[128,256]{1,0:T(8,128)(2,1)} %lc_w.1, bf16[256,128]{1,0:T(8,128)(2,1)} %proj_w.1, bf16[192,128]{1,0:T(8,128)(2,1)} %bitcast.5, bf16[8,192,256]{2,1,0:T(8,128)(2,1)} %bitcast.4), custom_call_target="tpu_custom_call" | custom-call | tf_op jit(solution)/shard_map/interaction_layer/pallas_call | solution.py:421
  34.0 2.3 %write_outputs.1 = (bf16[8,192,256]{2,1,0:T(8,128)(2,1)}, bf16[32,64,96]{2,1,0:T(8,128)(2,1)}, f32[128,256]{1,0:T(8,128)}, f32[256,128]{1,0:T(8,128)}, f32[192,128]{1,0:T(8,128)}) custom-call(bf16[8,192,256]{2,1,0:T(8,128)(2,1)} %get-tuple-element.13.layer, bf16[32,64,96]{2,1,0:T(8,128)(2,1)} %get-tuple-element.14.emb, ...), custom_call_target="tpu_custom_call" | custom-call | tf_op jit(solution)/shard_map/write_outputs/pallas_call | solution.py:433

commit v9 on v8

--- a/solution.py
+++ b/solution.py
@@ -105,6 +105,10 @@
                 x_copy(g, a, b).wait_recv()
             for j in range(1, tensors):
                 f_copy(g, a, j).start()
+        if g == rounds - 1:
+            for j in range(1, tensors):
+                for i in range(3):
+                    w_copy(i, j).start()
 
     def w_copy(i, j):
         src, dst = w_pairs[i]
@@ -119,9 +123,6 @@
                 x_copy(g, a, b).start()
     for c in range(chunks):
         c_copy(c).start()
-    for j in range(1, tensors):
-        for i in range(3):
-            w_copy(i, j).start()
 
     for load in w_loads:
         load.wait()

time: 36.5 us -> 38.5 us (1.055)
  Pallas kernels: 35.7 us -> 37.7 us
    pallas_call x1, Pallas kernels: 33.4 us -> 35.3 us  [shards(): pl.pallas_call(functools.partial(layer_kernel, cfg), out_shape=(layer_sha...]
where the time goes in v9:
time: 38.5 us; the launch traced here: 38.3 us
  Pallas kernels  37.7 us (98%)
  between operations  0.64 us (2%)
    pallas_call x1, Pallas kernels, shards(): pl.pallas_call(functools.partial(layer_kernel, cfg), out_shape=(layer_sha...  35.3 us
    pallas_call x1, Pallas kernels, shards(): pl.pallas_call(write_kernel, out_shape=(layer_shape, emb_shape, jax.Shape...  2.35 us

profile of v9, /device:TPU:0, one launch (start us, length us, event | category | flops | bytes accessed | tf_op | source)
XLA Modules:
  0.0 38.3 jit_solution(17020372184262197687)
XLA Ops:
  0.6 35.3 %interaction_layer.1 = (bf16[8,192,256]{2,1,0:T(8,128)(2,1)}, bf16[32,64,96]{2,1,0:T(8,128)(2,1)}, bf16[48,16,128]{2,1,0:T(8,128)(2,1)}) custom-call(bf16[32,64,192]{2,1,0:T(8,128)(2,1)} %pooled.1, bf16[128,256]{1,0:T(8,128)(2,1)} %lc_w.1, bf16[256,128]{1,0:T(8,128)(2,1)} %proj_w.1, bf16[192,128]{1,0:T(8,128)(2,1)} %bitcast.5, bf16[8,192,256]{2,1,0:T(8,128)(2,1)} %bitcast.4), custom_call_target="tpu_custom_call" | custom-call | tf_op jit(solution)/shard_map/interaction_layer/pallas_call | solution.py:422
  36.0 2.3 %write_outputs.1 = (bf16[8,192,256]{2,1,0:T(8,128)(2,1)}, bf16[32,64,96]{2,1,0:T(8,128)(2,1)}, f32[128,256]{1,0:T(8,128)}, f32[256,128]{1,0:T(8,128)}, f32[192,128]{1,0:T(8,128)}) custom-call(bf16[8,192,256]{2,1,0:T(8,128)(2,1)} %get-tuple-element.13.layer, bf16[32,64,96]{2,1,0:T(8,128)(2,1)} %get-tuple-element.14.emb, ...), custom_call_target="tpu_custom_call" | custom-call | tf_op jit(solution)/shard_map/write_outputs/pallas_call | solution.py:434
